TPU v7x, 256 devices: a whole 4x4x8 slice. The times are simulated.
256 devices in a mesh: batch: 4 (over x_lo, core), query: 64 (over y, z, x_hi).
Axes of the slice: x: 4 (x_hi: 2, x_lo: 2; x = x_hi * 2 + x_lo), y: 4, z: 8, core: 2. Of those that a mesh axis runs over, the one named last changes fastest.
Arguments:
- points: bfloat16 [4, 16384, 1024], P('batch', 'query'), may hold values from -100 to 100
- order: int32 [4, 64, 256], P('batch', 'query'), may hold values from 0 to 255, each once within a row
- cotangent: bfloat16 [4, 16384, 1024], P('batch', 'query'), may hold values from -6 to 6
- kv_cross: bfloat16 [4, 512, 2048], P('batch', 'query'), may hold values from -6 to 6
- self_qkv: bfloat16 [4, 512, 3072], P('batch', 'query'), may hold values from -400 to 400
- kv_weight: bfloat16 [1024, 2048], replicated, may hold values from -0.1875 to 0.1875
- out_weight: bfloat16 [1024, 1024], replicated, may hold values from -0.1875 to 0.1875
Outputs:
- grad_points: bfloat16 [4, 16384, 1024], P('batch', 'query')
- grad_latent: bfloat16 [4, 512, 1024], P('batch', 'query')
- grad_qkv: bfloat16 [4, 512, 3072], P('batch', 'query')
- grad_out_proj: float32 [1024, 1024], P('query')
Inputs may be any that keep to these rules, and one draw needn't show every extreme that they name: `order`: each row of 256 entries holds every number from 0 to 255 once.
All inputs are finite; a program needn't handle non-finite values.
Results may differ from a plain program's by a relative error of at most 0.015.
Values may be sent and summed in bfloat16 or wider, within the bound.
A program may use at most 128 MiB of HBM per device.

v0:
```python
import jax
import jax.numpy as jnp
from jax import lax
from jax.sharding import PartitionSpec as P

HEADS = 16


def inner(left, right):
    return lax.dot_general(
        left, right, (((1,), (1,)), ((), ())), preferred_element_type=jnp.float32
    )


def outer(left, right):
    return lax.dot_general(
        left, right, (((0,), (0,)), ((), ())), preferred_element_type=jnp.float32
    )


def project_exact(rows, weight_wide):
    return lax.dot_general(
        rows,
        weight_wide,
        (((1,), (1,)), ((), ())),
        precision=lax.Precision.HIGHEST,
        preferred_element_type=jnp.float32,
    )


def softmax_rows(scores):
    top = jnp.max(scores, axis=-1, keepdims=True)
    weights = jnp.exp(scores - top)
    return weights / jnp.sum(weights, axis=-1, keepdims=True)


def on_device(points, order, cotangent, kv_cross, self_qkv, kv_weight, out_weight):
    width = kv_weight.shape[0]
    head_size = width // HEADS
    rows_dev = points.shape[1]
    block = min(512, rows_dev)
    count = rows_dev // block
    scale = 1.0 / width**0.5
    sscale = 1.0 / head_size**0.5
    weight_wide = kv_weight.astype(jnp.float32)
    queries = points[0]
    grads_in = cotangent[0][order[0, 0]]
    cross_all, self_all = (
        lax.all_gather(kv_cross, "query", axis=1, tiled=True),
        lax.all_gather(self_qkv[:, :, width:], "query", axis=1, tiled=True),
    )
    keys = cross_all[0, :, :width]
    values = cross_all[0, :, width:]
    latents = keys.shape[0]
    owned = self_qkv.shape[1]
    query_blocks = queries.reshape(count, block, width)
    grad_blocks = grads_in.reshape(count, block, width)

    def cross_step(carry, items):
        qrows, grows = items
        probs = softmax_rows(inner(qrows, keys) * scale)
        dprob = inner(grows, values)
        delta = jnp.sum(probs * dprob, axis=-1, keepdims=True)
        dscore = (probs * (dprob - delta) * scale).astype(jnp.bfloat16)
        grad_rows = jnp.dot(dscore, keys, preferred_element_type=jnp.float32).astype(jnp.bfloat16)
        dkey = outer(dscore, qrows)
        dvalue = outer(probs.astype(jnp.bfloat16), grows)
        return ((carry[0] + dkey, carry[1] + dvalue), grad_rows)

    zero = jnp.zeros((latents, width), jnp.float32)
    (dkey_all, dvalue_all), grad_points = lax.scan(
        cross_step, (zero, zero), (query_blocks, grad_blocks)
    )
    terms = jnp.concatenate([dkey_all, dvalue_all], axis=1)
    summed = lax.psum_scatter(terms, "query", scatter_dimension=0, tiled=True)
    latent_grad = project_exact(summed, weight_wide).astype(jnp.bfloat16)
    q_own = self_qkv[0, :, :width].reshape(owned, HEADS, head_size)
    k_all = self_all[0, :, :width].reshape(latents, HEADS, head_size)
    v_all = self_all[0, :, width:].reshape(latents, HEADS, head_size)
    sprobs = softmax_rows(
        jnp.einsum("ihd,jhd->hij", q_own, k_all, preferred_element_type=jnp.float32) * sscale
    )
    sprobs_low = sprobs.astype(jnp.bfloat16)
    attended = jnp.einsum("hij,jhd->ihd", sprobs_low, v_all, preferred_element_type=jnp.float32)
    attended = attended.reshape(owned, width).astype(jnp.bfloat16)
    proj_term = outer(attended, latent_grad)
    proj_part = lax.psum_scatter(proj_term, "query", scatter_dimension=0, tiled=True)
    proj_grad = lax.psum(proj_part.astype(jnp.bfloat16), "batch").astype(jnp.float32)
    dattended = inner(latent_grad, out_weight).astype(jnp.bfloat16)
    dah = dattended.reshape(owned, HEADS, head_size)
    sdprob = jnp.einsum("ihd,jhd->hij", dah, v_all, preferred_element_type=jnp.float32)
    sdelta = jnp.sum(sprobs * sdprob, axis=-1, keepdims=True)
    sdscore = (sprobs * (sdprob - sdelta) * sscale).astype(jnp.bfloat16)
    dq_own = jnp.einsum("hij,jhd->ihd", sdscore, k_all, preferred_element_type=jnp.float32).reshape(
        owned, width
    )
    dk_all = jnp.einsum("hij,ihd->jhd", sdscore, q_own, preferred_element_type=jnp.float32).reshape(
        latents, width
    )
    dv_all = jnp.einsum(
        "hij,ihd->jhd", sprobs_low, dah, preferred_element_type=jnp.float32
    ).reshape(latents, width)
    dk_own, dv_own = (
        lax.psum_scatter(dk_all, "query", scatter_dimension=0, tiled=True),
        lax.psum_scatter(dv_all, "query", scatter_dimension=0, tiled=True),
    )
    grad_qkv = jnp.concatenate([dq_own, dk_own, dv_own], axis=1).astype(jnp.bfloat16)
    return (grad_points, latent_grad[None], grad_qkv[None], proj_grad)


def solution(mesh):
    placed = (
        P("batch", "query", None),
        P("batch", "query", None),
        P("batch", "query", None),
        P("batch", "query", None),
        P("batch", "query", None),
        P(),
        P(),
    )
    return jax.shard_map(
        on_device,
        mesh=mesh,
        in_specs=placed,
        out_specs=(
            P("batch", "query", None),
            P("batch", "query", None),
            P("batch", "query", None),
            P("query", None),
        ),
        check_vma=False,
    )
```

profile of v0, /device:TPU:39, one launch (start us, length us, event | category | flops | bytes accessed | tf_op | source)
XLA Modules:
  0.0 1724.7 jit_solution(14360416599799795550)
XLA Ops:
  7.2 0.0 copy-start
  7.2 0.0 all-gather.3.cloned.1.call-start
  7.2 0.7 all-gather.3.cloned.1.call-update
  7.9 0.0 all-gather.5.cloned.1.call-start
  8.0 1.4 slice.21
  9.3 0.0 all-gather.5.cloned.1.call-update
  9.4 0.0 reduce-scatter.5.cloned.1.call-start
  9.4 0.7 compare_select_fusion
  10.1 2.7 gather_fusion
  12.8 114.3 %all-gather.3.cloned.1.call-done = bf16[1,512,2048]{2,1,0:T(8,128)(2,1)} async-done(((bf16[1,8,2048]{2,1,0:T(8,128)(2,1)}), bf16[1,512,2048]{2,1,0:T(8,128)(2,1)}) %all-gather.3.cloned.1.call-update) | async-done | bytes 2097168 | tf_op jit(solution)/shard_map/all_gather | solution.py:49
  127.1 0.0 copy-start.4
  127.1 2.1 fusion.40
  129.2 0.2 fusion.21
  129.4 0.0 copy-done.4
  129.4 0.6 multiply_reduce_fusion
  130.0 0.0 copy-start.2
  130.0 0.0 copy-start.1
  130.0 0.6 fusion.22
  130.6 0.2 copy-done.2
  130.8 0.4 copy-done.1
  131.2 0.6 fusion.13
  131.9 2.4 pad_maximum_fusion
  134.3 0.0 slice-start
  134.3 0.0 reduce-scatter.5.cloned.1.call-update
  134.3 0.0 reduce-scatter.9.cloned.1.call-start
  134.4 0.6 slice-done
  135.0 0.1 reshape_squeeze.9
  135.1 111.6 %all-gather.5.cloned.1.call-done = bf16[1,512,2048]{2,1,0:T(8,128)(2,1)} async-done(((bf16[1,8,2048]{2,1,0:T(8,128)(2,1)}), bf16[1,512,2048]{2,1,0:T(8,128)(2,1)}) %all-gather.5.cloned.1.call-update) | async-done | bytes 2097168 | tf_op jit(solution)/shard_map/all_gather | solution.py:50
  246.7 3.1 fusion.39
  249.8 2.3 copy.17
  252.1 1.5 convolution_multiply_fusion.1
  253.6 2.7 fusion.41
  256.3 307.3 %reduce-scatter.5.cloned.1.call-done = f32[8,2048]{1,0:T(8,128)} async-done(((f32[512,2048]{1,0:T(8,128)}), f32[8,2048]{1,0:T(8,128)}) %reduce-scatter.5.cloned.1.call-update) | async-done | bytes 65552 | tf_op jit(solution)/shard_map/reduce_scatter | solution.py:75
  563.6 5.6 convolution_convert_fusion.4
  569.1 0.0 copy-done
  569.1 0.6 convolution_convert_fusion.3
  569.8 0.1 reshape.103
  569.9 1.9 fusion.27
  571.8 2.9 copy.25
  574.7 0.0 reduce-scatter.9.cloned.1.call-update
  574.8 0.0 reduce-scatter.7.cloned.1.call-start
  574.8 2.3 copy.19
  577.1 1.5 fusion.30
  578.6 2.2 fusion.12
  580.8 3.0 copy.23
  583.7 0.0 reduce-scatter.7.cloned.1.call-update
  583.7 0.0 reduce-scatter.11.cloned.1.call-start
  583.8 1.7 fusion.10
  585.5 0.1 convert_element_type.57
  585.6 0.0 copy-done.3
  585.6 2.7 fusion.42
  588.3 0.0 reduce-scatter.11.cloned.1.call-update
  588.3 2.7 fusion.2
  591.0 1.8 fusion.9
  592.8 0.1 concatenate.21
  592.9 338.5 %reduce-scatter.9.cloned.1.call-done = f32[8,1024]{1,0:T(8,128)} async-done(((f32[512,1024]{1,0:T(8,128)}), f32[8,1024]{1,0:T(8,128)}) %reduce-scatter.9.cloned.1.call-update) | async-done | bytes 32784 | tf_op jit(solution)/shard_map/reduce_scatter | solution.py:105
  931.4 0.8 convert_bitcast_fusion
  932.2 359.3 %reduce-scatter.7.cloned.1.call-done = f32[8,1024]{1,0:T(8,128)} async-done(((f32[512,1024]{1,0:T(8,128)}), f32[8,1024]{1,0:T(8,128)}) %reduce-scatter.7.cloned.1.call-update) | async-done | bytes 32784 | tf_op jit(solution)/shard_map/reduce_scatter | solution.py:104
  1291.5 0.8 convert_bitcast_fusion.1
  1292.3 0.6 pad_maximum_fusion.1
  1292.9 365.0 %reduce-scatter.11.cloned.1.call-done = f32[16,1024]{1,0:T(8,128)} async-done(((f32[1024,1024]{1,0:T(8,128)}), f32[16,1024]{1,0:T(8,128)}) %reduce-scatter.11.cloned.1.call-update) | async-done | bytes 65552 | tf_op jit(solution)/shard_map/reduce_scatter | solution.py:87
  1657.9 0.8 convert_element_type.58
  1658.7 58.5 %psum.7 = bf16[16,1024]{1,0:T(8,128)(2,1)S(1)} all-reduce(bf16[16,1024]{1,0:T(8,128)(2,1)S(1)} %convert_element_type.58), channel_id=1, replica_groups=mesh['batch'=4,'query'=64] {'batch'}, use_global_device_ids=true, to_apply=%region_10.11 | all-reduce | flops 16384 | bytes 65536 | tf_op jit(solution)/shard_map/psum | solution.py:88
  1717.2 0.6 convert_element_type.59
  (4 shorter events, 0.0 us)
Async XLA Ops:
  7.2 562.0 %copy-start = (bf16[1024,1024]{1,0:T(8,128)(2,1)S(1)}, bf16[1024,1024]{1,0:T(8,128)(2,1)}, u32[]{:S(2)}) copy-start(bf16[1024,1024]{1,0:T(8,128)(2,1)} %param.13) | copy-start | bytes 6291460
  7.2 119.9 %all-gather.3.cloned.1.call-start = ((), (), s32[]{:S(2)}) async-start(), calls=%async_computation.4 | async-start | bytes 2129920 | tf_op jit(solution)/shard_map/all_gather | solution.py:49
  7.9 238.8 %all-gather.5.cloned.1.call-start = ((), (), s32[]{:S(2)}) async-start(), calls=%async_computation.6 | async-start | bytes 2129920 | tf_op jit(solution)/shard_map/all_gather | solution.py:50
  9.4 554.2 %reduce-scatter.5.cloned.1.call-start = ((), (), s32[]{:S(2)}) async-start(), calls=%async_computation.5 | async-start | bytes 4259840 | tf_op jit(solution)/shard_map/reduce_scatter | solution.py:75
  127.1 2.3 copy-start.4
  130.0 0.8 copy-start.2
  130.0 1.2 copy-start.1
  134.3 0.7 slice-start
  134.3 797.1 %reduce-scatter.9.cloned.1.call-start = ((), (), s32[]{:S(2)}) async-start(), calls=%async_computation.8 | async-start | bytes 2129920 | tf_op jit(solution)/shard_map/reduce_scatter | solution.py:105
  569.1 16.5 copy-start.3
  574.8 716.7 %reduce-scatter.7.cloned.1.call-start = ((), (), s32[]{:S(2)}) async-start(), calls=%async_computation.7 | async-start | bytes 2129920 | tf_op jit(solution)/shard_map/reduce_scatter | solution.py:104
  583.7 1074.1 %reduce-scatter.11.cloned.1.call-start = ((), (), s32[]{:S(2)}) async-start(), calls=%async_computation.9 | async-start | bytes 4259840 | tf_op jit(solution)/shard_map/reduce_scatter | solution.py:87
Sparse Core Ops, SparseCore 0:
  11.6 115.4 all-gather.2
  131.3 115.3 all-gather.4
  249.2 314.2 reduce-scatter.4
  574.9 356.5 reduce-scatter.8
  933.8 357.6 reduce-scatter.6
  1294.0 363.7 reduce-scatter.10
where the time goes:
time: 1740 us; the launch traced here: 1720 us
  waiting for transfers between devices  1600 us (92%)
  blocking collectives  58.5 us (3%)
  matrix products  26 us (1%)
  local copies, waits for them, and re-layouts  19.3 us (1%)
    reduce_scatter x1, waiting for transfers between devices, on_device(): lax.psum_scatter(proj_term, 'query', scatter_dimension=0, tiled=True)  365 us
    reduce_scatter x1, waiting for transfers between devices, on_device(): lax.psum_scatter(dk_all, 'query', scatter_dimension=0, tiled=True)  359 us
    reduce_scatter x1, waiting for transfers between devices, on_device(): lax.psum_scatter(dv_all, 'query', scatter_dimension=0, tiled=True)  339 us
    reduce_scatter x1, waiting for transfers between devices, on_device(): summed = lax.psum_scatter(terms, 'query', scatter_dimension=0, tiled=True)  307 us
    all_gather x1, waiting for transfers between devices, on_device(): lax.all_gather(kv_cross, 'query', axis=1, tiled=True)  114 us
    all_gather x1, waiting for transfers between devices, on_device(): lax.all_gather(self_qkv[:, :, width:], 'query', axis=1, tiled=True)  112 us
    psum x1, blocking collectives, on_device(): lax.psum(proj_part.astype(jnp.bfloat16), 'batch').astype(jnp.float32)  58.5 us
  transfers between devices with their start and end apart: 6, of which 6 were waited for; matrix products, arithmetic and copies ran while one was open for 2% of the time, Pallas kernels for 0%

commit v1 on v0

v1 whole, which is shorter than its diff:
```python
import functools

import jax
import jax.numpy as jnp
from jax import lax
from jax.experimental import pallas as pl
from jax.experimental.pallas import tpu as pltpu
from jax.sharding import PartitionSpec as P

MESH = pl.DeviceIdType.MESH
BF = jnp.bfloat16
F32 = jnp.float32


def nt(a, b):
    return lax.dot_general(a, b, (((1,), (1,)), ((), ())), preferred_element_type=F32)


def nn(a, b):
    return lax.dot_general(a, b, (((1,), (0,)), ((), ())), preferred_element_type=F32)


def tn(a, b):
    return lax.dot_general(a, b, (((0,), (0,)), ((), ())), preferred_element_type=F32)


GROUPS = dict(
    kvrow=2, qy=3, qz=7, qx=2, swap_q=1, swap_g=1, kz0=7, ky1=3, kz1=7, ky0=3, sib0=4, sib1=8,
    pair=1, ry=3, rz=7, gz=7, gy=3, gsib=4, lat=1, proj=4, oz=3, oy=4, pts=1,
)
BASE = {}
COUNT = 0
for _name, _n in GROUPS.items():
    BASE[_name] = COUNT
    COUNT += _n


def kernel(
    points, order, cot, kv, sqkv, wkv, wo,
    gpts, glat, gqkv, gproj,
    gsend, qb, gb, kvs, kvr, kvf, sq, r1, r2, r3, wkvb, wob, qg, spt, sp16, att,
    psend, precv, pown, ysend, yrecv, zsend, zrecv, zacc, dzf, pjf, pjs, pjr,
    ob, or1, or2, gls, glr, gps,
    ss, rs, ls,
):
    b = lax.axis_index("batch")
    k = lax.axis_index("query")
    xlo = b // 2
    c = b % 2
    y = k // 16
    z = (k // 2) % 8
    xhi = k % 2
    swapped = c != xhi
    kept = c == xhi

    def dev(xlo_, c_, y_, z_, xhi_):
        return (xlo_ * 2 + c_, (y_ * 8 + z_) * 2 + xhi_)

    sib = dev(xlo, 1 - c, y, z, xhi)
    diag = dev(xlo, xhi, y, z, c)
    heads4 = z // 2

    def dev_y(j):
        return dev(xlo, c, (y + j) % 4, z, xhi)

    def dev_z(j):
        return dev(xlo, c, y, (z + j) % 8, xhi)

    def rc(src, dst, i, to):
        return pltpu.make_async_remote_copy(
            src_ref=src, dst_ref=dst, send_sem=ss.at[i], recv_sem=rs.at[i],
            device_id=to, device_id_type=MESH,
        )

    def at(name, j=0):
        return BASE[name] + j

    barrier = pltpu.get_barrier_semaphore()
    greet = [sib, dev(xlo, 1 - c, y, z, 1 - xhi), dev(xlo, c, y, z, 1 - xhi)]
    greet += [dev_y(j) for j in (1, 2, 3)] + [dev_z(j) for j in range(1, 8)]
    greet += [dev(xlo, 1 - c, (y + j) % 4, z, 1 - xhi) for j in (1, 2, 3)]
    greet += [dev(1 - xlo, cc, y, z, xx) for cc in (0, 1) for xx in (0, 1)]
    for to in greet:
        pl.semaphore_signal(barrier, inc=1, device_id=to, device_id_type=MESH)

    head = y * 4 + heads4
    load_w = pltpu.make_async_copy(wkv, wkvb, ls.at[0])
    load_w.start()
    load_o = pltpu.make_async_copy(wo.at[pl.ds(pl.multiple_of(head * 64, 64), 64)], wob, ls.at[1])
    load_o.start()

    kvw = kv[0].astype(F32)
    for t in (0, 1):
        kvs[t] = jnp.concatenate(
            [kvw[:, t * 1024:t * 1024 + 512], kvw[:, t * 1024 + 512:t * 1024 + 1024]], axis=0
        ).astype(BF)
    sw = sqkv[0].astype(F32)
    pad = jnp.zeros((8, 64), F32)
    for h in range(16):
        top = jnp.concatenate([sw[:, h * 64:h * 64 + 64], sw[:, 1024 + h * 64:1024 + h * 64 + 64]], axis=1)
        low = jnp.concatenate([sw[:, 2048 + h * 64:2048 + h * 64 + 64], pad], axis=1)
        sq[h] = jnp.concatenate([top, low], axis=0).astype(BF)
    hot = (lax.broadcasted_iota(jnp.int32, (256, 256), 0) == order[0]).astype(F32).astype(BF)
    gsend[...] = tn(hot, cot[0]).astype(BF)

    pl.semaphore_wait(barrier, len(greet))

    def kvrow(t):
        return rc(kvs.at[t], kvr.at[xhi], at("kvrow") + xhi, dev(xlo, t, y, z, c))

    def kvrow_send(t):
        return pltpu.make_async_remote_copy(
            src_ref=kvs.at[t], dst_ref=kvr.at[xhi], send_sem=ss.at[at("kvrow", t)],
            recv_sem=rs.at[at("kvrow") + xhi], device_id=dev(xlo, t, y, z, c), device_id_type=MESH,
        )

    local_row = pltpu.make_async_copy(kvs.at[c], kvr.at[xhi], ls.at[2])
    for t in (0, 1):
        mine = jnp.logical_and(kept, c == t)

        @pl.when(jnp.logical_not(mine))
        def _():
            kvrow_send(t).start()

    @pl.when(kept)
    def _():
        local_row.start()

    for j in (1, 2, 3):
        yj = (y + j) % 4
        rc(sq.at[pl.ds(yj * 4, 4)], r1.at[y], at("qy", j - 1), dev_y(j)).start()
    local_qy = pltpu.make_async_copy(sq.at[pl.ds(y * 4, 4)], r1.at[y], ls.at[3])
    local_qy.start()

    swap_q = rc(points.at[0], qb, at("swap_q"), diag)
    local_q = pltpu.make_async_copy(points.at[0], qb, ls.at[4])
    swap_g = rc(gsend, gb, at("swap_g"), diag)
    local_g = pltpu.make_async_copy(gsend, gb, ls.at[5])

    @pl.when(swapped)
    def _():
        swap_q.start()
        swap_g.start()

    @pl.when(kept)
    def _():
        local_q.start()
        local_g.start()

    for blk in (0, 1):
        mine = jnp.logical_and(kept, xhi == blk)

        @pl.when(jnp.logical_not(mine))
        def _():
            rc(kvs.at[0], kvr.at[blk], at("kvrow", blk), sib).wait_recv()

    @pl.when(kept)
    def _():
        local_row.wait()

    p0 = kvr[0].astype(F32)
    p1 = kvr[1].astype(F32)
    kvf[c, 0, y, z] = jnp.concatenate([p0[:8], p1[:8]], axis=0).astype(BF)
    kvf[c, 1, y, z] = jnp.concatenate([p0[8:], p1[8:]], axis=0).astype(BF)

    def kz0(j, slot):
        return rc(kvf.at[c, 0, y, slot], kvf.at[c, 0, y, slot], at("kz0", j - 1), dev_z(j))

    def ky1(j, slot):
        return rc(kvf.at[c, 1, slot, z], kvf.at[c, 1, slot, z], at("ky1", j - 1), dev_y(j))

    def kz1(j, slot):
        return rc(kvf.at[c, 1, :, slot], kvf.at[c, 1, :, slot], at("kz1", j - 1), dev_z(j))

    def ky0(j, slot):
        return rc(kvf.at[c, 0, slot], kvf.at[c, 0, slot], at("ky0", j - 1), dev_y(j))

    def sib0(which, j, slot):
        return rc(kvf.at[which, 0, slot], kvf.at[which, 0, slot], at("sib0", j), sib)

    def sib1(which, j, slot):
        return rc(kvf.at[which, 1, :, slot], kvf.at[which, 1, :, slot], at("sib1", j), sib)

    for j in (1, 2, 3):
        ky1(j, y).start()
    for j in range(1, 8):
        kz0(j, z).start()

    for j in (1, 2, 3):
        rc(r1.at[0], r1.at[(y + 4 - j) % 4], at("qy", j - 1), sib).wait_recv()
    local_qy.wait()
    for j in range(1, 8):
        zj = (z + j) % 8
        rc(r1.at[:, zj // 2], r2.at[:, z], at("qz", j - 1), dev_z(j)).start()
    local_qz = pltpu.make_async_copy(r1.at[:, heads4], r2.at[:, z], ls.at[6])
    local_qz.start()

    for j in (1, 2, 3):
        ky1(j, (y + 4 - j) % 4).wait_recv()
    for j in range(1, 8):
        kz1(j, z).start()
    sib1(c, 0, z).start()

    for j in range(1, 8):
        rc(r1.at[:, 0], r2.at[:, (z + 8 - j) % 8], at("qz", j - 1), sib).wait_recv()
    local_qz.wait()

    def qx_send(t):
        return pltpu.make_async_remote_copy(
            src_ref=r2, dst_ref=r3.at[:, :, xhi], send_sem=ss.at[at("qx", t)],
            recv_sem=rs.at[at("qx") + xhi], device_id=dev(xlo, t, y, z, c), device_id_type=MESH,
        )

    local_qx = pltpu.make_async_copy(r2, r3.at[:, :, xhi], ls.at[7])
    for t in (0, 1):
        mine = jnp.logical_and(kept, c == t)

        @pl.when(jnp.logical_not(mine))
        def _():
            qx_send(t).start()

    @pl.when(kept)
    def _():
        local_qx.start()

    for j in range(1, 8):
        kz0(j, (z + 8 - j) % 8).wait_recv()
    for j in (1, 2, 3):
        ky0(j, y).start()
    sib0(c, 0, y).start()

    load_w.wait()

    @pl.when(swapped)
    def _():
        swap_q.wait_recv()

    @pl.when(kept)
    def _():
        local_q.wait()

    qw = nt(qb[...], wkvb[:, 0:1024]).astype(BF)
    qg[0, 0:256] = qw[:, 0:512]
    qg[1, 0:256] = qw[:, 512:1024]

    for blk in (0, 1):
        mine = jnp.logical_and(kept, xhi == blk)

        @pl.when(jnp.logical_not(mine))
        def _():
            rc(r2, r3.at[:, :, blk], at("qx", blk), sib).wait_recv()

    @pl.when(kept)
    def _():
        local_qx.wait()

    tiles = r3[...].astype(F32).reshape(64, 16, 128)
    top = tiles[:, :8].reshape(512, 128)
    low = tiles[:, 8:].reshape(512, 128)
    sq_q = top[:, :64].astype(BF)
    sq_k = top[:, 64:].astype(BF)
    sq_v = low[:, :64].astype(BF)
    sscale = 1.0 / 64 ** 0.5
    scores = nt(sq_k, sq_q) * sscale
    weights = jnp.exp(scores - jnp.max(scores, axis=0, keepdims=True))
    sprobs = weights / jnp.sum(weights, axis=0, keepdims=True)
    spt[...] = sprobs
    sp16[...] = sprobs.astype(BF)
    vt = low[:, :64].T.astype(BF)
    att[...] = nn(vt, sp16[...]).astype(BF)

    for j in range(1, 8):
        kz1(j, (z + 8 - j) % 8).wait_recv()
        sib1(c, j, (z + 8 - j) % 8).start()
    for j in (1, 2, 3):
        ky0(j, (y + 4 - j) % 4).wait_recv()
        sib0(c, j, (y + 4 - j) % 4).start()

    @pl.when(swapped)
    def _():
        swap_g.wait_recv()

    @pl.when(kept)
    def _():
        local_g.wait()

    gw = nt(gb[...], wkvb[:, 1024:2048]).astype(BF)
    qg[0, 256:512] = gw[:, 0:512]
    qg[1, 256:512] = gw[:, 512:1024]

    for j in range(8):
        sib1(1 - c, j, (z + 8 - j) % 8).wait_recv()
    for j in range(4):
        sib0(1 - c, j, (y + 4 - j) % 4).wait_recv()

    def half(t, h):
        return kvf[t, h].reshape(512, 512)

    scale = 1.0 / 1024 ** 0.5
    s = (nt(half(0, 0), qb[:, 0:512]) + nt(half(0, 1), qb[:, 512:1024])) * scale
    e = jnp.exp(s - jnp.max(s, axis=0, keepdims=True))
    p = e / jnp.sum(e, axis=0, keepdims=True)
    dp = nt(half(1, 0), gb[:, 0:512]) + nt(half(1, 1), gb[:, 512:1024])
    delta = jnp.sum(p * dp, axis=0, keepdims=True)
    ds = (p * (dp - delta) * scale).astype(BF)
    both = jnp.concatenate([ds, p.astype(BF)], axis=1)

    psend[...] = nn(both, qg[1 - c]).astype(BF).reshape(4, 128, 512)
    pair = rc(psend, precv, at("pair"), sib)
    pair.start()
    pown[...] = nn(both, qg[c]).reshape(4, 128, 512)
    gps[:, 0:512] = tn(ds, half(0, 0)).astype(BF)
    gps[:, 512:1024] = tn(ds, half(0, 1)).astype(BF)
    pts = rc(gps, gpts.at[0], at("pts"), diag)
    local_pts = pltpu.make_async_copy(gps, gpts.at[0], ls.at[8])
    pair.wait_recv()

    @pl.when(swapped)
    def _():
        pts.start()

    @pl.when(kept)
    def _():
        local_pts.start()

    for j in (1, 2, 3):
        yj = (y + j) % 4
        ysend[j - 1] = (pown[yj] + precv[yj].astype(F32)).astype(BF)
        rc(ysend.at[j - 1], yrecv.at[j - 1], at("ry", j - 1), dev_y(j)).start()
    acc = pown[y] + precv[y].astype(F32)
    for j in (1, 2, 3):
        rc(ysend.at[j - 1], yrecv.at[j - 1], at("ry", j - 1), dev_y(j)).wait_recv()
        acc = acc + yrecv[j - 1].astype(F32)
    zacc[...] = acc.reshape(8, 16, 512)
    zsend[...] = acc.astype(BF).reshape(8, 16, 512)
    for j in range(1, 8):
        rc(zsend.at[(z + j) % 8], zrecv.at[j - 1], at("rz", j - 1), dev_z(j)).start()
    acc = zacc[z]
    for j in range(1, 8):
        rc(zsend.at[j], zrecv.at[j - 1], at("rz", j - 1), dev_z(j)).wait_recv()
        acc = acc + zrecv[j - 1].astype(F32)
    dzf[c, y, z] = acc.astype(BF)

    def gz(j, slot):
        return rc(dzf.at[c, y, slot], dzf.at[c, y, slot], at("gz", j - 1), dev_z(j))

    def gy(j, slot):
        return rc(dzf.at[c, slot], dzf.at[c, slot], at("gy", j - 1), dev_y(j))

    def gsib(which, j, slot):
        return rc(dzf.at[which, slot], dzf.at[which, slot], at("gsib", j), sib)

    for j in range(1, 8):
        gz(j, z).start()
    for j in range(1, 8):
        gz(j, (z + 8 - j) % 8).wait_recv()
    for j in (1, 2, 3):
        gy(j, y).start()
    gsib(c, 0, y).start()
    for j in (1, 2, 3):
        gy(j, (y + 4 - j) % 4).wait_recv()
        gsib(c, j, (y + 4 - j) % 4).start()
    for j in range(4):
        gsib(1 - c, j, (y + 4 - j) % 4).wait_recv()

    load_o.wait()
    dz0 = dzf[0].reshape(512, 512)
    dz1 = dzf[1].reshape(512, 512)
    datt = (nt(dz0, wob[:, 0:512]) + nt(dz1, wob[:, 512:1024])).astype(BF)
    pjf[:, 0:512] = nn(att[...], dz0)
    pjf[:, 512:1024] = nn(att[...], dz1)
    pjs[...] = pjf[pl.ds(pl.multiple_of(((z % 2) * 2 + c) * 16, 16), 16), :].astype(BF)

    shape_at = xlo * 2 + xhi

    def proj_send(a, t):
        return pltpu.make_async_remote_copy(
            src_ref=pjs, dst_ref=pjr.at[shape_at], send_sem=ss.at[at("proj", a * 2 + t)],
            recv_sem=rs.at[at("proj") + shape_at], device_id=dev(a, t, y, z, c), device_id_type=MESH,
        )

    local_proj = pltpu.make_async_copy(pjs, pjr.at[shape_at], ls.at[9])

    def proj_mine(a, t):
        return jnp.logical_and(kept, jnp.logical_and(xlo == a, c == t))

    for a in (0, 1):
        for t in (0, 1):

            @pl.when(jnp.logical_not(proj_mine(a, t)))
            def _():
                proj_send(a, t).start()

    own0 = dzf[0, y, z].astype(F32)
    own1 = dzf[1, y, z].astype(F32)
    first = c == 0
    gls[...] = jnp.concatenate(
        [jnp.where(first, own0[:8], own0[8:]), jnp.where(first, own1[:8], own1[8:])], axis=0
    ).astype(BF)
    lat = rc(gls, glr, at("lat"), diag)
    local_lat = pltpu.make_async_copy(gls, glr, ls.at[10])

    @pl.when(swapped)
    def _():
        lat.start()

    @pl.when(kept)
    def _():
        local_proj.start()
        local_lat.start()

    sdp = nt(sq_v, datt)
    sprobs = spt[...]
    sdelta = jnp.sum(sprobs * sdp, axis=0, keepdims=True)
    sds = (sprobs * (sdp - sdelta) * sscale).astype(BF)
    dk = nn(sds, sq_q)
    dv = nn(sp16[...], datt)
    kt = top[:, 64:].T.astype(BF)
    dq = nn(kt, sds).T
    m1 = jnp.concatenate([dq, dk], axis=1).reshape(64, 8, 128)
    m2 = jnp.concatenate([dv, jnp.zeros((512, 64), F32)], axis=1).reshape(64, 8, 128)
    ob[...] = jnp.concatenate([m1, m2], axis=1).astype(BF).reshape(4, 8, 2, 16, 128)

    for j in (1, 2, 3):
        zj = (z + 2 * j) % 8
        rc(ob.at[:, zj, c], or1.at[heads4], at("oz", j - 1), dev_z(2 * j)).start()
    local_oz = pltpu.make_async_copy(ob.at[:, z, c], or1.at[heads4], ls.at[11])
    local_oz.start()
    for j in (1, 2, 3):
        rc(ob.at[:, 0, 0], or1.at[(heads4 + 4 - j) % 4], at("oz", j - 1), sib).wait_recv()
    local_oz.wait()

    def oy(j):
        yj = (y + j) % 4
        return rc(or1.at[:, yj], or2.at[y], at("oy", j), dev(xlo, xhi, yj, z, c))

    for j in (1, 2, 3):
        oy(j).start()
    local_oy = pltpu.make_async_copy(or1.at[:, y], or2.at[y], ls.at[12])

    @pl.when(swapped)
    def _():
        oy(0).start()

    @pl.when(kept)
    def _():
        local_oy.start()

    for src in range(4):

        @pl.when(jnp.logical_not(jnp.logical_and(kept, shape_at == src)))
        def _():
            rc(pjs, pjr.at[src], at("proj", src), sib).wait_recv()

    @pl.when(kept)
    def _():
        local_proj.wait()
        local_lat.wait()
        local_pts.wait()

    @pl.when(swapped)
    def _():
        lat.wait_recv()
        pts.wait_recv()

    total = pjr[0].astype(F32)
    for src in (1, 2, 3):
        total = total + pjr[src].astype(F32)
    gproj[...] = total
    lr = glr[...].astype(F32)
    glat[0] = jnp.concatenate([lr[:8], lr[8:]], axis=1).astype(BF)

    for j in (1, 2, 3):
        rc(or1.at[:, 0], or2.at[(y + 4 - j) % 4], at("oy", j), sib).wait_recv()

    @pl.when(swapped)
    def _():
        oy(0).wait_recv()

    @pl.when(kept)
    def _():
        local_oy.wait()

    res = or2[...].astype(F32).reshape(16, 16, 128)
    parts = [res[h, :8, 0:64] for h in range(16)]
    parts += [res[h, :8, 64:128] for h in range(16)]
    parts += [res[h, 8:, 0:64] for h in range(16)]
    gqkv[0] = jnp.concatenate(parts, axis=1).astype(BF)

    for t in (0, 1):
        mine = jnp.logical_and(kept, c == t)

        @pl.when(jnp.logical_not(mine))
        def _():
            kvrow_send(t).wait_send()
            qx_send(t).wait_send()

    for j in (1, 2, 3):
        rc(sq.at[pl.ds(0, 4)], r1.at[y], at("qy", j - 1), sib).wait_send()
        ky1(j, y).wait_send()
        ky0(j, y).wait_send()
        rc(ysend.at[j - 1], yrecv.at[j - 1], at("ry", j - 1), sib).wait_send()
        gy(j, y).wait_send()
        rc(ob.at[:, 0, 0], or1.at[0], at("oz", j - 1), sib).wait_send()
        oy(j).wait_send()
    for j in range(1, 8):
        kz0(j, z).wait_send()
        kz1(j, z).wait_send()
        rc(r1.at[:, 0], r2.at[:, z], at("qz", j - 1), sib).wait_send()
        rc(zsend.at[j], zrecv.at[j - 1], at("rz", j - 1), sib).wait_send()
        gz(j, z).wait_send()
    for j in range(8):
        sib1(c, j, (z + 8 - j) % 8).wait_send()
    for j in range(4):
        sib0(c, j, (y + 4 - j) % 4).wait_send()
        gsib(c, j, (y + 4 - j) % 4).wait_send()
    pair.wait_send()
    for a in (0, 1):
        for t in (0, 1):

            @pl.when(jnp.logical_not(proj_mine(a, t)))
            def _():
                proj_send(a, t).wait_send()

    @pl.when(swapped)
    def _():
        swap_q.wait_send()
        swap_g.wait_send()
        pts.wait_send()
        lat.wait_send()
        oy(0).wait_send()


def on_device(points, order, cotangent, kv_cross, self_qkv, kv_weight, out_weight):
    vmem = pl.BlockSpec(memory_space=pltpu.VMEM)
    hbm = pl.BlockSpec(memory_space=pl.ANY)
    scratch = [
        ((256, 1024), BF),
        ((256, 1024), BF),
        ((256, 1024), BF),
        ((2, 16, 512), BF),
        ((2, 16, 512), BF),
        ((2, 2, 4, 8, 16, 512), BF),
        ((16, 16, 128), BF),
        ((4, 4, 16, 128), BF),
        ((4, 8, 16, 128), BF),
        ((4, 8, 2, 16, 128), BF),
        ((1024, 2048), BF),
        ((64, 1024), BF),
        ((2, 512, 512), BF),
        ((512, 512), F32),
        ((512, 512), BF),
        ((64, 512), BF),
        ((4, 128, 512), BF),
        ((4, 128, 512), BF),
        ((4, 128, 512), F32),
        ((3, 128, 512), BF),
        ((3, 128, 512), BF),
        ((8, 16, 512), BF),
        ((7, 16, 512), BF),
        ((8, 16, 512), F32),
        ((2, 4, 8, 16, 512), BF),
        ((64, 1024), F32),
        ((16, 1024), BF),
        ((4, 16, 1024), BF),
        ((4, 8, 2, 16, 128), BF),
        ((4, 4, 16, 128), BF),
        ((4, 4, 16, 128), BF),
        ((16, 512), BF),
        ((16, 512), BF),
        ((256, 1024), BF),
    ]
    return pl.pallas_call(
        kernel,
        out_shape=(
            jax.ShapeDtypeStruct((1, 256, 1024), BF),
            jax.ShapeDtypeStruct((1, 8, 1024), BF),
            jax.ShapeDtypeStruct((1, 8, 3072), BF),
            jax.ShapeDtypeStruct((16, 1024), F32),
        ),
        in_specs=[hbm, vmem, vmem, vmem, vmem, hbm, hbm],
        out_specs=(vmem, vmem, vmem, vmem),
        scratch_shapes=[pltpu.VMEM(shape, dtype) for shape, dtype in scratch]
        + [pltpu.SemaphoreType.DMA((COUNT,)), pltpu.SemaphoreType.DMA((COUNT,)), pltpu.SemaphoreType.DMA((13,))],
        name="fused_backward",
        cost_estimate=pl.CostEstimate(flops=3_000_000_000, bytes_accessed=8_000_000, transcendentals=400_000),
        compiler_params=pltpu.CompilerParams(
            collective_id=0, has_side_effects=True, vmem_limit_bytes=56 * 1024 * 1024
        ),
    )(points, order, cotangent, kv_cross, self_qkv, kv_weight, out_weight)


def solution(mesh):
    rows = P("batch", "query", None)
    return jax.shard_map(
        on_device,
        mesh=mesh,
        in_specs=(rows, rows, rows, rows, rows, P(), P()),
        out_specs=(rows, rows, rows, P("query", None)),
        check_vma=False,
    )
```

time: 1740 us -> 85 us (0.05)
  the two profiles are of different devices: /device:TPU:39 before, /device:TPU:1 now
where the time goes in v1:
time: 85 us; the launch traced here: 84.7 us
  Pallas kernels  77.9 us (92%)
  local copies, waits for them, and re-layouts  6.08 us (7%)
    pallas_call x1, Pallas kernels, on_device(): pl.pallas_call(kernel, out_shape=(jax.ShapeDtypeStruct((1, 256, 1024), BF...  77.9 us
    unnamed x4, local copies, waits for them, and re-layouts  6.08 us

profile of v1, /device:TPU:1, one launch (start us, length us, event | category | flops | bytes accessed | tf_op | source)
XLA Modules:
  0.0 84.7 jit_solution(11333793812405537830)
XLA Ops:
  0.6 77.9 %fused_backward.1 = (bf16[1,256,1024]{2,1,0:T(8,128)(2,1)}, bf16[1,8,1024]{2,1,0:T(8,128)(2,1)}, bf16[1,8,3072]{2,1,0:T(8,128)(2,1)}, f32[16,1024]{1,0:T(8,128)}) custom-call(bf16[1,256,1024]{2,1,0:T(8,128)(2,1)} %points.1, s32[1,1,256]{2,1,0:T(1,128)} %order.1, bf16[1,256,1024]{2,1,0:T(8,128)(2,1)} %cot.1, bf16[1,8,2048]{2,1,0:T(8,128)(2,1)} %kv.1, ...), custom_call_target="tpu_custom_call" | custom-call | flops 3000000000 | bytes 8000000 | tf_op jit(solution)/shard_map/fused_backward/pallas_call | solution.py:573
  78.6 1.9 %copy.15 = bf16[1,256,1024]{2,1,0:T(8,128)(2,1)} copy(bf16[1,256,1024]{2,1,0:T(8,128)(2,1)} %get-tuple-element.8) | data formatting | bytes 1048576
  80.4 1.3 %copy.16 = bf16[1,8,1024]{2,1,0:T(8,128)(2,1)} copy(bf16[1,8,1024]{2,1,0:T(8,128)(2,1)} %get-tuple-element.9) | data formatting | bytes 32768
  81.8 1.4 %copy.17 = bf16[1,8,3072]{2,1,0:T(8,128)(2,1)} copy(bf16[1,8,3072]{2,1,0:T(8,128)(2,1)} %get-tuple-element.10) | data formatting | bytes 98304
  83.2 1.5 %copy.18 = f32[16,1024]{1,0:T(8,128)} copy(f32[16,1024]{1,0:T(8,128)} %get-tuple-element.11) | data formatting | bytes 131072

commit v2 on v0

v2 whole, which is shorter than its diff:
```python
import functools

import jax
import jax.numpy as jnp
from jax import lax
from jax.experimental import pallas as pl
from jax.experimental.pallas import tpu as pltpu
from jax.sharding import PartitionSpec as P

MESH = pl.DeviceIdType.MESH
BF = jnp.bfloat16
F32 = jnp.float32


def nt(a, b):
    return lax.dot_general(a, b, (((1,), (1,)), ((), ())), preferred_element_type=F32)


def nn(a, b):
    return lax.dot_general(a, b, (((1,), (0,)), ((), ())), preferred_element_type=F32)


def tn(a, b):
    return lax.dot_general(a, b, (((0,), (0,)), ((), ())), preferred_element_type=F32)


GROUPS = dict(
    kvrow=2, qy=3, qz=7, qx=2, swap_q=1, swap_g=1, kz=7, ky=24, ks=4,
    pair=4, ry=24, rz=7, gz=7, gy=24, gs=4, lat=1, proj=4, back=16, pts=1,
)
MIX_Z = (4, 1, 7, 2, 6, 3, 5)
FAR_Z = (4, 3, 5, 2, 6, 1, 7)
NEAR_Z = (1, 7, 2, 6, 3, 5, 4)
ARRIVE_Z = (1, 7, 2, 6, 4, 3, 5)
FAR_Y = (2, 1, 3)
NEAR_ROWS = (0, 1, 7, 2)
BASE = {}
COUNT = 0
for _name, _n in GROUPS.items():
    BASE[_name] = COUNT
    COUNT += _n


def kernel(
    points, order, cot, kv, sqkv, wkv, wo,
    gpts, or2, glr, pjr,
    cotb, gsend, qb, gb, kvs, kvr, kv16, sq, r1, r2, r3, wkvb, wob, qg, spt, spi, att, ot, oti,
    pboth, psend, precv, pown, ysend, yrecv, zsend, zrecv, dz,
    dat, pjf, pjs, ob, gls, gps,
    ss, rs, ls,
):
    b = lax.axis_index("batch")
    k = lax.axis_index("query")
    xlo = b // 2
    c = b % 2
    y = k // 16
    z = (k // 2) % 8
    xhi = k % 2
    swapped = c != xhi
    kept = c == xhi

    def dev(xlo_, c_, y_, z_, xhi_):
        return (xlo_ * 2 + c_, (y_ * 8 + z_) * 2 + xhi_)

    sib = dev(xlo, 1 - c, y, z, xhi)
    diag = dev(xlo, xhi, y, z, c)
    z4 = z % 4
    zt = 2 * z4 + z // 4
    zs = z // 2 + 4 * (z % 2)
    same = jnp.logical_and(kept, z == zt)

    def dev_y(j):
        return dev(xlo, c, (y + j) % 4, z, xhi)

    def dev_z(j):
        return dev(xlo, c, y, (z + j) % 8, xhi)

    def yb(j):
        return (y + 4 - j) % 4

    def zb(j):
        return (z + 8 - j) % 8

    def back_to(j, i):
        return dev(xlo, xhi, (y + j) % 4, (z + i) % 8, c)

    def on(when, fn):
        if when is None:
            fn()
        else:
            pl.when(when)(fn)

    sends, arrivals, locals_ = [], {}, {}

    def go(name, j, src, dst, to, arrive, when=None, rj=None):
        i = BASE[name] + j
        copy = pltpu.make_async_remote_copy(
            src_ref=src, dst_ref=dst, send_sem=ss.at[i],
            recv_sem=rs.at[i if rj is None else BASE[name] + rj],
            device_id=to, device_id_type=MESH,
        )
        on(when, copy.start)
        sends.append((copy, when))
        here = pltpu.make_async_remote_copy(
            src_ref=arrive, dst_ref=arrive, send_sem=ss.at[i], recv_sem=rs.at[i],
            device_id=sib, device_id_type=MESH,
        )
        arrivals[name, j] = (here, when)

    def got(name, j=0):
        here, when = arrivals.pop((name, j))
        on(when, here.wait_recv)

    def local(i, src, dst, when=None):
        copy = pltpu.make_async_copy(src, dst, ls.at[i])
        on(when, copy.start)
        locals_[i] = (copy, when)

    def got_local(i):
        copy, when = locals_.pop(i)
        on(when, copy.wait)

    def drain():
        for i in list(locals_):
            got_local(i)
        for name, j in list(arrivals):
            got(name, j)
        for copy, when in sends:
            on(when, copy.wait_send)

    barrier = pltpu.get_barrier_semaphore()
    greet = [sib, dev(xlo, 1 - c, y, z, 1 - xhi), dev(xlo, c, y, z, 1 - xhi)]
    greet += [dev_y(j) for j in (1, 2, 3)] + [dev_z(j) for j in range(1, 8)]
    greet += [back_to(j, i) for j in range(4) for i in range(8) if i in NEAR_ROWS + (6,) and (j, i) != (0, 0)]
    for to in greet:
        pl.semaphore_signal(barrier, inc=1, device_id=to, device_id_type=MESH)

    def far(a, t):
        return jnp.logical_not(jnp.logical_and(same, jnp.logical_and(xlo == a, xhi == t)))

    for a in (0, 1):
        for t in (0, 1):

            @pl.when(jnp.logical_not(jnp.logical_and(same, jnp.logical_and(xlo == a, c == t))))
            def _():
                pl.semaphore_signal(barrier, inc=1, device_id=dev(a, t, y, zt, c), device_id_type=MESH)

            @pl.when(far(a, t))
            def _():
                pl.semaphore_signal(barrier, inc=1, device_id=dev(a, xhi, y, zs, t), device_id_type=MESH)

    head = y * 4 + z4
    local(13, cot.at[0], cotb)
    local(0, wkv, wkvb)
    local(1, wo.at[pl.ds(pl.multiple_of(head * 64, 64), 64)], wob)

    kvw = kv[0].astype(F32)
    for t in (0, 1):
        kvs[t] = jnp.concatenate(
            [kvw[:, t * 1024:t * 1024 + 512], kvw[:, t * 1024 + 512:t * 1024 + 1024]], axis=0
        ).astype(BF)
    pl.semaphore_wait(barrier, len(greet) + 8 - 2 * same.astype(jnp.int32))

    mine = [jnp.logical_and(kept, c == t) for t in (0, 1)]
    other = [jnp.logical_not(m) for m in mine]
    for t in (0, 1):
        go("kvrow", t, kvs.at[t], kvr.at[xhi], dev(xlo, t, y, z, c), kvr.at[t], when=other[t], rj=xhi)
    local(2, kvs.at[c], kvr.at[xhi], when=kept)
    go("swap_q", 0, points.at[0], qb, diag, qb, when=swapped)
    local(4, points.at[0], qb, when=kept)
    sw = sqkv[0].astype(F32)
    pad = jnp.zeros((8, 64), F32)
    for h in range(16):
        top = jnp.concatenate([sw[:, h * 64:h * 64 + 64], sw[:, 1024 + h * 64:1024 + h * 64 + 64]], axis=1)
        low = jnp.concatenate([sw[:, 2048 + h * 64:2048 + h * 64 + 64], pad], axis=1)
        sq[h] = jnp.concatenate([top, low], axis=0).astype(BF)
    for j in FAR_Y:
        go("qy", j - 1, sq.at[pl.ds((y + j) % 4 * 4, 4)], r1.at[y], dev_y(j), r1.at[yb(j)])
    local(3, sq.at[pl.ds(y * 4, 4)], r1.at[y])
    hot = (lax.broadcasted_iota(jnp.int32, (256, 256), 0) == order[0]).astype(F32).astype(BF)
    got_local(13)
    gsend[...] = tn(hot, cotb[...]).astype(BF)

    go("swap_g", 0, gsend, gb, diag, gb, when=swapped)
    local(5, gsend, gb, when=kept)

    got("kvrow", 0)
    got("kvrow", 1)
    got_local(2)
    p0 = kvr[0].astype(F32)
    p1 = kvr[1].astype(F32)
    left = jnp.concatenate([p0[:8], p1[:8]], axis=0)
    right = jnp.concatenate([p0[8:], p1[8:]], axis=0)
    kv16[c, y, z] = jnp.concatenate([left, right], axis=1).astype(BF)
    for i in FAR_Y:
        go("ky", i - 1, kv16.at[c, y, z], kv16.at[c, y, z], dev_y(i), kv16.at[c, yb(i), z])
    for j in MIX_Z:
        go("kz", j - 1, kv16.at[c, y, z], kv16.at[c, y, z], dev_z(j), kv16.at[c, y, zb(j)])

    def on_along_y(j):
        got("kz", j - 1)
        slot = zb(j)
        for i in FAR_Y:
            go("ky", j * 3 + i - 1, kv16.at[c, y, slot], kv16.at[c, y, slot], dev_y(i), kv16.at[c, yb(i), slot])

    for j in ARRIVE_Z[:2]:
        on_along_y(j)

    for j in (1, 2, 3):
        got("qy", j - 1)
    got_local(3)
    for j in FAR_Z:
        go("qz", j - 1, r1.at[:, (z + j) % 4], r2.at[:, z], dev_z(j), r2.at[:, zb(j)])
    local(6, r1.at[:, z4], r2.at[:, z])

    for j in ARRIVE_Z[2:]:
        on_along_y(j)
    go("ks", 0, kv16.at[c, y], kv16.at[c, y], sib, kv16.at[1 - c, y])

    got_local(0)
    got("swap_q")
    got_local(4)
    qw = nt(qb[...], wkvb[:, 0:1024]).astype(BF)
    qg[0, 0:256] = qw[:, 0:512]
    qg[1, 0:256] = qw[:, 512:1024]

    got("swap_g")
    got_local(5)
    gw = nt(gb[...], wkvb[:, 1024:2048]).astype(BF)
    qg[0, 256:512] = gw[:, 0:512]
    qg[1, 256:512] = gw[:, 512:1024]

    for j in range(1, 8):
        got("qz", j - 1)
    got_local(6)
    for t in (0, 1):
        go("qx", t, r2, r3.at[:, :, xhi], dev(xlo, t, y, z, c), r3.at[:, :, t], when=other[t], rj=xhi)
    local(7, r2, r3.at[:, :, xhi], when=kept)

    for i in (1, 3, 2):
        for j in range(8):
            got("ky", j * 3 + i - 1)
        slot = yb(i)
        go("ks", i, kv16.at[c, slot], kv16.at[c, slot], sib, kv16.at[1 - c, slot])
    for j in range(4):
        got("ks", j)

    keys = kv16[0].reshape(512, 1024)
    values = kv16[1].reshape(512, 1024)
    scale = 1.0 / 1024 ** 0.5
    s = nt(keys, qb[...]) * scale
    e = jnp.exp(s - jnp.max(s, axis=0, keepdims=True))
    p = e / jnp.sum(e, axis=0, keepdims=True)
    dp = nt(values, gb[...])
    delta = jnp.sum(p * dp, axis=0, keepdims=True)
    ds = (p * (dp - delta) * scale).astype(BF)
    pboth[...] = jnp.concatenate([ds, p.astype(BF)], axis=1).reshape(4, 128, 512)

    for i in FAR_Y + (0,):
        yi = (y + i) % 4
        psend[yi] = nn(pboth[yi], qg[1 - c]).astype(BF).reshape(8, 16, 512)
        go("pair", i, psend.at[yi], precv.at[yi], sib, precv.at[yi])
    for i in FAR_Y + (0,):
        yi = (y + i) % 4
        pown[yi] = nn(pboth[yi], qg[c]).reshape(8, 16, 512)
    for i in FAR_Y:
        yi = (y + i) % 4
        got("pair", i)
        for j in FAR_Z + (0,):
            zj = (z + j) % 8
            ysend[j, i - 1] = (pown[yi, zj] + precv[yi, zj].astype(F32)).astype(BF)
            go("ry", j * 3 + i - 1, ysend.at[j, i - 1], yrecv.at[j, i - 1], dev_y(i), yrecv.at[j, i - 1])

    gps[...] = tn(ds, kv16[0].reshape(512, 1024)).astype(BF)
    got("qx", 0)
    got("qx", 1)
    got_local(7)
    go("pts", 0, gps, gpts.at[0], diag, gpts.at[0], when=swapped)
    local(8, gps, gpts.at[0], when=kept)
    tiles = r3[...].astype(F32).reshape(64, 16, 128)
    top = tiles[:, :8].reshape(512, 128)
    low = tiles[:, 8:].reshape(512, 128)
    sq_q = top[:, :64].astype(BF)
    sq_k = top[:, 64:].astype(BF)
    sq_v = low[:, :64].astype(BF)
    kt = top[:, 64:].T.astype(BF)
    vt = low[:, :64].T.astype(BF)

    def near_rows(ref):
        return jnp.concatenate([ref[:, (z + i) % 8, c].astype(F32) for i in NEAR_ROWS], axis=0)

    own = near_rows(r3)
    own_q = own[:, :8].reshape(128, 128)[:, :64].astype(BF)
    own_v = own[:, 8:].reshape(128, 128)[:, :64].astype(BF)
    sscale = 1.0 / 64 ** 0.5

    def columns_softmax(scores):
        weights = jnp.exp(scores - jnp.max(scores, axis=0, keepdims=True))
        return weights / jnp.sum(weights, axis=0, keepdims=True)

    def attend(probs):
        high = probs.astype(BF)
        rounded = nn(vt, high)
        return rounded, rounded + nn(vt, (probs - high.astype(F32)).astype(BF))

    sprobs = columns_softmax(nt(sq_k, sq_q) * sscale)
    spt[...] = sprobs.reshape(4, 8, 2, 8, 512)
    attended, ot[...] = attend(sprobs)
    att[...] = attended.astype(BF)
    sprobs = columns_softmax(nt(sq_k, own_q) * sscale)
    spi[...] = sprobs
    _, oti[...] = attend(sprobs)

    got("pair", 0)
    for j in FAR_Z + (0,):
        zj = (z + j) % 8
        acc = pown[y, zj] + precv[y, zj].astype(F32)
        for i in FAR_Y:
            got("ry", j * 3 + i - 1)
            acc = acc + yrecv[j, i - 1].astype(F32)
        if j:
            zsend[j - 1] = acc.astype(BF)
            go("rz", j - 1, zsend.at[j - 1], zrecv.at[j - 1], dev_z(j), zrecv.at[j - 1])
    for j in range(1, 8):
        got("rz", j - 1)
        acc = acc + zrecv[j - 1].astype(F32)
    dz[c, y, z] = acc.astype(BF)

    for j in MIX_Z:
        go("gz", j - 1, dz.at[c, y, z], dz.at[c, y, z], dev_z(j), dz.at[c, y, zb(j)])
    for i in FAR_Y:
        go("gy", i - 1, dz.at[c, y, z], dz.at[c, y, z], dev_y(i), dz.at[c, yb(i), z])
    for j in ARRIVE_Z:
        got("gz", j - 1)
        slot = zb(j)
        for i in FAR_Y:
            go("gy", j * 3 + i - 1, dz.at[c, y, slot], dz.at[c, y, slot], dev_y(i), dz.at[c, yb(i), slot])
    go("gs", 0, dz.at[c, y], dz.at[c, y], sib, dz.at[1 - c, y])
    for i in (1, 3, 2):
        for j in range(8):
            got("gy", j * 3 + i - 1)
        slot = yb(i)
        go("gs", i, dz.at[c, slot], dz.at[c, slot], sib, dz.at[1 - c, slot])
    for i in range(4):
        got("gs", i)

    got_local(1)
    dz0 = dz[0].reshape(512, 512)
    dz1 = dz[1].reshape(512, 512)
    datt = nt(dz0, wob[:, 0:512]) + nt(dz1, wob[:, 512:1024])
    datt = datt.astype(BF)
    dattw = datt.astype(F32)
    dat[...] = dattw.reshape(4, 8, 2, 8, 64)
    own_datt = near_rows(dat).reshape(128, 64)
    sdelta = jnp.sum(dattw.T * ot[...], axis=0, keepdims=True)
    own_sdelta = jnp.sum(own_datt.T * oti[...], axis=0, keepdims=True)
    rows_p = near_rows(spt).reshape(128, 512)
    sds = (rows_p * (nt(own_v, datt) - sdelta) * sscale).astype(BF)
    dk = nn(sds, sq_q)
    dv = nn(rows_p.astype(BF), datt)
    sds = (spi[...] * (nt(sq_v, own_datt.astype(BF)) - own_sdelta) * sscale).astype(BF)
    dq = nn(kt, sds).T
    m1 = jnp.concatenate([dq, dk], axis=1).reshape(16, 8, 128)
    m2 = jnp.concatenate([dv, jnp.zeros((128, 64), F32)], axis=1).reshape(16, 8, 128)
    ob[...] = jnp.concatenate([m1, m2], axis=1).astype(BF).reshape(4, 4, 16, 128)

    for at, i in reversed(list(enumerate(NEAR_ROWS))):
        for j in (2, 1, 3, 0):
            go("back", j * 4 + at, ob.at[at, (y + j) % 4], or2.at[y, z4], back_to(j, i),
               or2.at[yb(j), (z + 8 - i) % 4], when=None if j + i else swapped)
    local(11, ob.at[0, y], or2.at[y, z4], when=kept)

    pjf[:, 0:512] = nn(att[...], dz0)
    pjf[:, 512:1024] = nn(att[...], dz1)
    pjs[...] = pjf[pl.ds(pl.multiple_of((z // 4 * 2 + c) * 16, 16), 16), :].astype(BF)
    shape_at = xlo * 2 + xhi
    for a in (0, 1):
        for t in (0, 1):
            away = jnp.logical_not(jnp.logical_and(same, jnp.logical_and(xlo == a, c == t)))
            go("proj", a * 2 + t, pjs, pjr.at[shape_at], dev(a, t, y, zt, c), pjr.at[a * 2 + t], when=away, rj=shape_at)
    local(9, pjs, pjr.at[shape_at], when=same)

    rows = [dz[t, y, z].astype(F32) for t in (0, 1)]
    first = c == 0
    gls[...] = jnp.concatenate([jnp.where(first, r[:8], r[8:]) for r in rows], axis=0).astype(BF)
    go("lat", 0, gls, glr, diag, glr, when=swapped)
    local(10, gls, glr, when=kept)
    drain()


def finish(pts, or2, glr, pjr, gpts, glat, gqkv, gproj, held, sem):
    into = pltpu.make_async_copy(pts, held, sem.at[0])
    into.start()
    into.wait()
    out = pltpu.make_async_copy(held, gpts, sem.at[1])
    out.start()
    total = pjr[0].astype(F32)
    for src in (1, 2, 3):
        total = total + pjr[src].astype(F32)
    gproj[...] = total
    lr = glr[...].astype(F32)
    glat[0] = jnp.concatenate([lr[:8], lr[8:]], axis=1).astype(BF)
    res = or2[...].astype(F32).reshape(16, 16, 128)
    parts = [res[h, :8, 0:64] for h in range(16)]
    parts += [res[h, :8, 64:128] for h in range(16)]
    parts += [res[h, 8:, 0:64] for h in range(16)]
    gqkv[0] = jnp.concatenate(parts, axis=1).astype(BF)
    out.wait()


def on_device(points, order, cotangent, kv_cross, self_qkv, kv_weight, out_weight):
    vmem = pl.BlockSpec(memory_space=pltpu.VMEM)
    hbm = pl.BlockSpec(memory_space=pl.ANY)
    scratch = [
        ((256, 1024), BF),
        ((256, 1024), BF),
        ((256, 1024), BF),
        ((256, 1024), BF),
        ((2, 16, 512), BF),
        ((2, 16, 512), BF),
        ((2, 4, 8, 16, 1024), BF),
        ((16, 16, 128), BF),
        ((4, 4, 16, 128), BF),
        ((4, 8, 16, 128), BF),
        ((4, 8, 2, 16, 128), BF),
        ((1024, 2048), BF),
        ((64, 1024), BF),
        ((2, 512, 512), BF),
        ((4, 8, 2, 8, 512), F32),
        ((512, 128), F32),
        ((64, 512), BF),
        ((64, 512), F32),
        ((64, 128), F32),
        ((4, 128, 512), BF),
        ((4, 8, 16, 512), BF),
        ((4, 8, 16, 512), BF),
        ((4, 8, 16, 512), F32),
        ((8, 3, 16, 512), BF),
        ((8, 3, 16, 512), BF),
        ((7, 16, 512), BF),
        ((7, 16, 512), BF),
        ((2, 4, 8, 16, 512), BF),
        ((4, 8, 2, 8, 64), F32),
        ((64, 1024), F32),
        ((16, 1024), BF),
        ((4, 4, 16, 128), BF),
        ((16, 512), BF),
        ((256, 1024), BF),
    ]
    parts = pl.pallas_call(
        kernel,
        out_shape=(
            jax.ShapeDtypeStruct((1, 256, 1024), BF),
            jax.ShapeDtypeStruct((4, 4, 16, 128), BF),
            jax.ShapeDtypeStruct((16, 512), BF),
            jax.ShapeDtypeStruct((4, 16, 1024), BF),
        ),
        in_specs=[hbm, vmem, hbm, vmem, vmem, hbm, hbm],
        out_specs=(hbm, hbm, hbm, hbm),
        scratch_shapes=[pltpu.VMEM(shape, dtype) for shape, dtype in scratch]
        + [pltpu.SemaphoreType.DMA((COUNT,)), pltpu.SemaphoreType.DMA((COUNT,)), pltpu.SemaphoreType.DMA((14,))],
        name="fused_backward",
        cost_estimate=pl.CostEstimate(flops=3_000_000_000, bytes_accessed=8_000_000, transcendentals=400_000),
        compiler_params=pltpu.CompilerParams(
            collective_id=0, has_side_effects=True, vmem_limit_bytes=56 * 1024 * 1024
        ),
    )(points, order, cotangent, kv_cross, self_qkv, kv_weight, out_weight)
    return pl.pallas_call(
        finish,
        out_shape=(
            jax.ShapeDtypeStruct((1, 256, 1024), BF),
            jax.ShapeDtypeStruct((1, 8, 1024), BF),
            jax.ShapeDtypeStruct((1, 8, 3072), BF),
            jax.ShapeDtypeStruct((16, 1024), F32),
        ),
        in_specs=[hbm, vmem, vmem, vmem],
        out_specs=(hbm, vmem, vmem, vmem),
        scratch_shapes=[pltpu.VMEM((1, 256, 1024), BF), pltpu.SemaphoreType.DMA((2,))],
        name="finish",
        cost_estimate=pl.CostEstimate(flops=100_000, bytes_accessed=1_500_000, transcendentals=0),
    )(*parts)


def solution(mesh):
    rows = P("batch", "query", None)
    return jax.shard_map(
        on_device,
        mesh=mesh,
        in_specs=(rows, rows, rows, rows, rows, P(), P()),
        out_specs=(rows, rows, rows, P("query", None)),
        check_vma=False,
    )
```

time: 1740 us -> 75.4 us (0.04)
  waiting for transfers between devices: 1600 us -> 0 us
  Pallas kernels: 0 us -> 74.6 us
  blocking collectives: 58.5 us -> 0 us
  matrix products: 26 us -> 0 us
  local copies, waits for them, and re-layouts: 19.3 us -> 0 us
    reduce_scatter x4 -> x0, waiting for transfers between devices: 1370 us -> none  [the longest x1 365 us: on_device(): lax.psum_scatter(proj_term, 'query', scatter_dimension=0, tiled=True)]
    all_gather x2 -> x0, waiting for transfers between devices: 226 us -> none  [the longest x1 114 us: on_device(): lax.all_gather(kv_cross, 'query', axis=1, tiled=True)]
    pallas_call x0 -> x2, Pallas kernels: none -> 74.6 us  [the longest x1 71.1 us: on_device(): pl.pallas_call(kernel, out_shape=(jax.ShapeDtypeStruct((1, 256, 1024), BF...]
    psum x1 -> x0, blocking collectives: 58.5 us -> none  [on_device(): lax.psum(proj_part.astype(jnp.bfloat16), 'batch').astype(jnp.float32)]
    dot_general x14 -> x0, matrix products: 26 us -> none  [the longest x1 5.57 us: project_exact(): lax.dot_general(rows, weight_wide, (((1,), (1,)), ((), ())), precision=la...]
  transfers between devices with their start and end apart: 6 -> 0, of which waited for: 6 -> 0; matrix products, arithmetic and copies ran while one was open for 2% -> 0% of each run, Pallas kernels for 0% -> 0%
where the time goes in v2:
time: 75.4 us; the launch traced here: 75.2 us
  Pallas kernels  74.6 us (99%)
    pallas_call x1, Pallas kernels, on_device(): pl.pallas_call(kernel, out_shape=(jax.ShapeDtypeStruct((1, 256, 1024), BF...  71.1 us
    pallas_call x1, Pallas kernels, on_device(): pl.pallas_call(finish, out_shape=(jax.ShapeDtypeStruct((1, 256, 1024), BF...  3.46 us

profile of v2, /device:TPU:39, one launch (start us, length us, event | category | flops | bytes accessed | tf_op | source)
XLA Modules:
  0.0 75.2 jit_solution(8151986530651947468)
XLA Ops:
  0.6 71.1 %fused_backward.1 = (bf16[1,256,1024]{2,1,0:T(8,128)(2,1)}, bf16[4,4,16,128]{3,2,1,0:T(8,128)(2,1)}, bf16[16,512]{1,0:T(8,128)(2,1)}, bf16[4,16,1024]{2,1,0:T(8,128)(2,1)}) custom-call(bf16[1,256,1024]{2,1,0:T(8,128)(2,1)} %points.1, s32[1,1,256]{2,1,0:T(1,128)} %order.1, bf16[1,256,1024]{2,1,0:T(8,128)(2,1)} %cot.1, bf16[1,8,2048]{2,1,0:T(8,128)(2,1)} %kv.1, ...), custom_call_target="tpu_custom_call" | custom-call | flops 3000000000 | bytes 8000000 | tf_op jit(solution)/shard_map/fused_backward/pallas_call | solution.py:450
  71.7 3.5 %finish.1 = (bf16[1,256,1024]{2,1,0:T(8,128)(2,1)}, bf16[1,8,1024]{2,1,0:T(8,128)(2,1)}, bf16[1,8,3072]{2,1,0:T(8,128)(2,1)}, f32[16,1024]{1,0:T(8,128)}) custom-call(bf16[1,256,1024]{2,1,0:T(8,128)(2,1)} %get-tuple-element.8.pts, bf16[4,4,16,128]{3,2,1,0:T(8,128)(2,1)} %get-tuple-element.9.or2, bf16[16,512]{1,0:T(8,128)(2,1)} %get-tuple-element.10.glr, ...), custom_call_target="tpu_custom_call" | custom-call | flops 100000 | bytes 1500000 | tf_op jit(solution)/shard_map/finish/pallas_call | solution.py:468

commit v3 on v2

--- a/solution.py
+++ b/solution.py
@@ -25,9 +25,10 @@
 
 
 GROUPS = dict(
-    kvrow=2, qy=3, qz=7, qx=2, swap_q=1, swap_g=1, kz=7, ky=24, ks=4,
+    kvrow=2, qy=3, qz=7, qx=2, swap_q=1, swap_g=1, kz=7, ky=3, ks=1, kyb=3, kzb=7, ksb=1,
     pair=4, ry=24, rz=7, gz=7, gy=24, gs=4, lat=1, proj=4, back=16, pts=1,
 )
+KA, KB = 768, 256
 MIX_Z = (4, 1, 7, 2, 6, 3, 5)
 FAR_Z = (4, 3, 5, 2, 6, 1, 7)
 NEAR_Z = (1, 7, 2, 6, 3, 5, 4)
@@ -42,9 +43,9 @@
 
 
 def kernel(
-    points, order, cot, kv, sqkv, wkv, wo,
+    points, order_in, cot, kv_in, sqkv_in, wkv, wo,
     gpts, or2, glr, pjr,
-    cotb, gsend, qb, gb, kvs, kvr, kv16, sq, r1, r2, r3, wkvb, wob, qg, spt, spi, att, ot, oti,
+    order, kv, sqkv, cotb, gsend, qgb, kvs, kvr, kv16, kvb, sq, r1, r2, r3, wkvb, wob, qg, spt, spi, att, ot, oti,
     pboth, psend, precv, pown, ysend, yrecv, zsend, zrecv, dz,
     dat, pjf, pjs, ob, gls, gps,
     ss, rs, ls,
@@ -92,21 +93,35 @@
 
     sends, arrivals, locals_ = [], {}, {}
 
-    def go(name, j, src, dst, to, arrive, when=None, rj=None):
+    def go(name, j, src, dst, to, arrive, when=None, rj=None, together=False):
         i = BASE[name] + j
         copy = pltpu.make_async_remote_copy(
-            src_ref=src, dst_ref=dst, send_sem=ss.at[i],
+            src_ref=src, dst_ref=dst, send_sem=ss.at[BASE[name] if together else i],
             recv_sem=rs.at[i if rj is None else BASE[name] + rj],
             device_id=to, device_id_type=MESH,
         )
         on(when, copy.start)
-        sends.append((copy, when))
+        if not together:
+            sends.append((copy, when))
+        if arrive is not None:
+            all_here(name, j, arrive, when)
+
+    def all_here(name, j, arrive, when=None):
+        i = BASE[name] + j
         here = pltpu.make_async_remote_copy(
             src_ref=arrive, dst_ref=arrive, send_sem=ss.at[i], recv_sem=rs.at[i],
             device_id=sib, device_id_type=MESH,
         )
         arrivals[name, j] = (here, when)
 
+    def all_sent(name, total):
+        i = BASE[name]
+        copy = pltpu.make_async_remote_copy(
+            src_ref=total, dst_ref=total, send_sem=ss.at[i], recv_sem=rs.at[i],
+            device_id=sib, device_id_type=MESH,
+        )
+        sends.append((copy, None))
+
     def got(name, j=0):
         here, when = arrivals.pop((name, j))
         on(when, here.wait_recv)
@@ -125,8 +140,12 @@
             got_local(i)
         for name, j in list(arrivals):
             got(name, j)
+        leave()
+
+    def leave():
         for copy, when in sends:
             on(when, copy.wait_send)
+        sends.clear()
 
     barrier = pltpu.get_barrier_semaphore()
     greet = [sib, dev(xlo, 1 - c, y, z, 1 - xhi), dev(xlo, c, y, z, 1 - xhi)]
@@ -149,11 +168,15 @@
             def _():
                 pl.semaphore_signal(barrier, inc=1, device_id=dev(a, xhi, y, zs, t), device_id_type=MESH)
 
+    local(14, kv_in, kv)
+    local(15, sqkv_in, sqkv)
+    local(16, order_in, order)
     head = y * 4 + z4
     local(13, cot.at[0], cotb)
     local(0, wkv, wkvb)
     local(1, wo.at[pl.ds(pl.multiple_of(head * 64, 64), 64)], wob)
 
+    got_local(14)
     kvw = kv[0].astype(F32)
     for t in (0, 1):
         kvs[t] = jnp.concatenate(
@@ -166,8 +189,9 @@
     for t in (0, 1):
         go("kvrow", t, kvs.at[t], kvr.at[xhi], dev(xlo, t, y, z, c), kvr.at[t], when=other[t], rj=xhi)
     local(2, kvs.at[c], kvr.at[xhi], when=kept)
-    go("swap_q", 0, points.at[0], qb, diag, qb, when=swapped)
-    local(4, points.at[0], qb, when=kept)
+    go("swap_q", 0, points.at[0], qgb.at[0], diag, qgb.at[0], when=swapped)
+    local(4, points.at[0], qgb.at[0], when=kept)
+    got_local(15)
     sw = sqkv[0].astype(F32)
     pad = jnp.zeros((8, 64), F32)
     for h in range(16):
@@ -175,14 +199,17 @@
         low = jnp.concatenate([sw[:, 2048 + h * 64:2048 + h * 64 + 64], pad], axis=1)
         sq[h] = jnp.concatenate([top, low], axis=0).astype(BF)
     for j in FAR_Y:
-        go("qy", j - 1, sq.at[pl.ds((y + j) % 4 * 4, 4)], r1.at[y], dev_y(j), r1.at[yb(j)])
+        go("qy", j - 1, sq.at[pl.ds((y + j) % 4 * 4, 4)], r1.at[y], dev_y(j), None, rj=0, together=True)
+    all_here("qy", 0, r1.at[pl.ds(0, 3)])
+    all_sent("qy", r1.at[pl.ds(0, 3)])
     local(3, sq.at[pl.ds(y * 4, 4)], r1.at[y])
+    got_local(16)
     hot = (lax.broadcasted_iota(jnp.int32, (256, 256), 0) == order[0]).astype(F32).astype(BF)
     got_local(13)
     gsend[...] = tn(hot, cotb[...]).astype(BF)
 
-    go("swap_g", 0, gsend, gb, diag, gb, when=swapped)
-    local(5, gsend, gb, when=kept)
+    go("swap_g", 0, gsend, qgb.at[1], diag, qgb.at[1], when=swapped)
+    local(5, gsend, qgb.at[1], when=kept)
 
     got("kvrow", 0)
     got("kvrow", 1)
@@ -191,67 +218,84 @@
     p1 = kvr[1].astype(F32)
     left = jnp.concatenate([p0[:8], p1[:8]], axis=0)
     right = jnp.concatenate([p0[8:], p1[8:]], axis=0)
-    kv16[c, y, z] = jnp.concatenate([left, right], axis=1).astype(BF)
+    kv16[c, y, z] = jnp.concatenate([left, right[:, :KA - 512]], axis=1).astype(BF)
+    kvb[c, y, z] = right[:, KA - 512:].astype(BF)
     for i in FAR_Y:
-        go("ky", i - 1, kv16.at[c, y, z], kv16.at[c, y, z], dev_y(i), kv16.at[c, yb(i), z])
+        go("ky", i - 1, kv16.at[c, y, z], kv16.at[c, y, z], dev_y(i), None, together=True)
     for j in MIX_Z:
-        go("kz", j - 1, kv16.at[c, y, z], kv16.at[c, y, z], dev_z(j), kv16.at[c, y, zb(j)])
+        go("kz", j - 1, kv16.at[c, y, z], kv16.at[c, y, z], dev_z(j), kv16.at[c, y, zb(j)], together=True)
+    all_sent("kz", kv16.at[0, 0, pl.ds(0, 7)])
 
     def on_along_y(j):
         got("kz", j - 1)
         slot = zb(j)
         for i in FAR_Y:
-            go("ky", j * 3 + i - 1, kv16.at[c, y, slot], kv16.at[c, y, slot], dev_y(i), kv16.at[c, yb(i), slot])
-
-    for j in ARRIVE_Z[:2]:
+            go("ky", i - 1, kv16.at[c, y, slot], kv16.at[c, y, slot], dev_y(i), None, together=True)
+
+    for i in FAR_Y:
+        go("kyb", i - 1, kvb.at[c, y, z], kvb.at[c, y, z], dev_y(i), kvb.at[c, yb(i), z], together=True)
+    all_sent("kyb", kvb.at[0, 0, pl.ds(0, 3)])
+    for j in ARRIVE_Z[:4]:
         on_along_y(j)
-
     for j in (1, 2, 3):
-        got("qy", j - 1)
+        got("kyb", j - 1)
+    for j in FAR_Z:
+        go("kzb", j - 1, kvb.at[c, :, z], kvb.at[c, :, z], dev_z(j), None, rj=0, together=True)
+    all_here("kzb", 0, kvb.at[c, :, pl.ds(0, 7)])
+    all_sent("kzb", kvb.at[c, :, pl.ds(0, 7)])
+    for j in ARRIVE_Z[4:]:
+        on_along_y(j)
+    got("qy")
     got_local(3)
     for j in FAR_Z:
-        go("qz", j - 1, r1.at[:, (z + j) % 4], r2.at[:, z], dev_z(j), r2.at[:, zb(j)])
+        go("qz", j - 1, r1.at[:, (z + j) % 4], r2.at[:, z], dev_z(j), None, rj=0, together=True)
+    all_here("qz", 0, r2.at[:, pl.ds(0, 7)])
+    all_sent("qz", r2.at[:, pl.ds(0, 7)])
     local(6, r1.at[:, z4], r2.at[:, z])
 
-    for j in ARRIVE_Z[2:]:
-        on_along_y(j)
-    go("ks", 0, kv16.at[c, y], kv16.at[c, y], sib, kv16.at[1 - c, y])
+    all_sent("ky", kv16.at[0, pl.ds(0, 3)])
+    go("ks", 0, kv16.at[c, y], kv16.at[c, y], sib, None, together=True)
 
     got_local(0)
     got("swap_q")
     got_local(4)
-    qw = nt(qb[...], wkvb[:, 0:1024]).astype(BF)
+    qw = nt(qgb[0], wkvb[:, 0:1024]).astype(BF)
     qg[0, 0:256] = qw[:, 0:512]
     qg[1, 0:256] = qw[:, 512:1024]
 
     got("swap_g")
     got_local(5)
-    gw = nt(gb[...], wkvb[:, 1024:2048]).astype(BF)
+    gw = nt(qgb[1], wkvb[:, 1024:2048]).astype(BF)
     qg[0, 256:512] = gw[:, 0:512]
     qg[1, 256:512] = gw[:, 512:1024]
 
-    for j in range(1, 8):
-        got("qz", j - 1)
+    got("kzb")
+    go("ksb", 0, kvb.at[c], kvb.at[c], sib, kvb.at[1 - c])
+    for i in (1, 3, 2):
+        slot = yb(i)
+        all_here("ky", i - 1, kv16.at[c, slot])
+        got("ky", i - 1)
+        go("ks", 0, kv16.at[c, slot], kv16.at[c, slot], sib, None, together=True)
+    all_here("ks", 0, kv16.at[1 - c])
+    all_sent("ks", kv16.at[c])
+    got("qz")
     got_local(6)
     for t in (0, 1):
         go("qx", t, r2, r3.at[:, :, xhi], dev(xlo, t, y, z, c), r3.at[:, :, t], when=other[t], rj=xhi)
     local(7, r2, r3.at[:, :, xhi], when=kept)
 
-    for i in (1, 3, 2):
-        for j in range(8):
-            got("ky", j * 3 + i - 1)
-        slot = yb(i)
-        go("ks", i, kv16.at[c, slot], kv16.at[c, slot], sib, kv16.at[1 - c, slot])
-    for j in range(4):
-        got("ks", j)
-
-    keys = kv16[0].reshape(512, 1024)
-    values = kv16[1].reshape(512, 1024)
+    def product(t):
+        return nt(kv16[t].reshape(512, KA), qgb[t, :, 0:KA]) + nt(kvb[t].reshape(512, KB), qgb[t, :, KA:1024])
+
+    mine_first = product(c)
+    got("ksb")
+    got("ks")
+    then = product(1 - c)
     scale = 1.0 / 1024 ** 0.5
-    s = nt(keys, qb[...]) * scale
+    s = jnp.where(c == 0, mine_first, then) * scale
     e = jnp.exp(s - jnp.max(s, axis=0, keepdims=True))
     p = e / jnp.sum(e, axis=0, keepdims=True)
-    dp = nt(values, gb[...])
+    dp = jnp.where(c == 0, then, mine_first)
     delta = jnp.sum(p * dp, axis=0, keepdims=True)
     ds = (p * (dp - delta) * scale).astype(BF)
     pboth[...] = jnp.concatenate([ds, p.astype(BF)], axis=1).reshape(4, 128, 512)
@@ -259,58 +303,24 @@
     for i in FAR_Y + (0,):
         yi = (y + i) % 4
         psend[yi] = nn(pboth[yi], qg[1 - c]).astype(BF).reshape(8, 16, 512)
-        go("pair", i, psend.at[yi], precv.at[yi], sib, precv.at[yi])
+        go("pair", i, psend.at[yi], precv.at[yi], sib, precv.at[yi], together=True)
     for i in FAR_Y + (0,):
         yi = (y + i) % 4
         pown[yi] = nn(pboth[yi], qg[c]).reshape(8, 16, 512)
+    all_sent("pair", psend)
     for i in FAR_Y:
         yi = (y + i) % 4
         got("pair", i)
         for j in FAR_Z + (0,):
             zj = (z + j) % 8
             ysend[j, i - 1] = (pown[yi, zj] + precv[yi, zj].astype(F32)).astype(BF)
-            go("ry", j * 3 + i - 1, ysend.at[j, i - 1], yrecv.at[j, i - 1], dev_y(i), yrecv.at[j, i - 1])
-
-    gps[...] = tn(ds, kv16[0].reshape(512, 1024)).astype(BF)
-    got("qx", 0)
-    got("qx", 1)
-    got_local(7)
+            go("ry", j * 3 + i - 1, ysend.at[j, i - 1], yrecv.at[j, i - 1], dev_y(i), yrecv.at[j, i - 1], together=True)
+    all_sent("ry", ysend)
+
+    gps[:, 0:KA] = tn(ds, kv16[0].reshape(512, KA)).astype(BF)
+    gps[:, KA:1024] = tn(ds, kvb[0].reshape(512, KB)).astype(BF)
     go("pts", 0, gps, gpts.at[0], diag, gpts.at[0], when=swapped)
     local(8, gps, gpts.at[0], when=kept)
-    tiles = r3[...].astype(F32).reshape(64, 16, 128)
-    top = tiles[:, :8].reshape(512, 128)
-    low = tiles[:, 8:].reshape(512, 128)
-    sq_q = top[:, :64].astype(BF)
-    sq_k = top[:, 64:].astype(BF)
-    sq_v = low[:, :64].astype(BF)
-    kt = top[:, 64:].T.astype(BF)
-    vt = low[:, :64].T.astype(BF)
-
-    def near_rows(ref):
-        return jnp.concatenate([ref[:, (z + i) % 8, c].astype(F32) for i in NEAR_ROWS], axis=0)
-
-    own = near_rows(r3)
-    own_q = own[:, :8].reshape(128, 128)[:, :64].astype(BF)
-    own_v = own[:, 8:].reshape(128, 128)[:, :64].astype(BF)
-    sscale = 1.0 / 64 ** 0.5
-
-    def columns_softmax(scores):
-        weights = jnp.exp(scores - jnp.max(scores, axis=0, keepdims=True))
-        return weights / jnp.sum(weights, axis=0, keepdims=True)
-
-    def attend(probs):
-        high = probs.astype(BF)
-        rounded = nn(vt, high)
-        return rounded, rounded + nn(vt, (probs - high.astype(F32)).astype(BF))
-
-    sprobs = columns_softmax(nt(sq_k, sq_q) * sscale)
-    spt[...] = sprobs.reshape(4, 8, 2, 8, 512)
-    attended, ot[...] = attend(sprobs)
-    att[...] = attended.astype(BF)
-    sprobs = columns_softmax(nt(sq_k, own_q) * sscale)
-    spi[...] = sprobs
-    _, oti[...] = attend(sprobs)
-
     got("pair", 0)
     for j in FAR_Z + (0,):
         zj = (z + j) % 8
@@ -320,29 +330,71 @@
             acc = acc + yrecv[j, i - 1].astype(F32)
         if j:
             zsend[j - 1] = acc.astype(BF)
-            go("rz", j - 1, zsend.at[j - 1], zrecv.at[j - 1], dev_z(j), zrecv.at[j - 1])
+            go("rz", j - 1, zsend.at[j - 1], zrecv.at[j - 1], dev_z(j), None, rj=0, together=True)
+    all_here("rz", 0, zrecv)
+    all_sent("rz", zsend)
+    got("rz")
     for j in range(1, 8):
-        got("rz", j - 1)
         acc = acc + zrecv[j - 1].astype(F32)
     dz[c, y, z] = acc.astype(BF)
 
     for j in MIX_Z:
-        go("gz", j - 1, dz.at[c, y, z], dz.at[c, y, z], dev_z(j), dz.at[c, y, zb(j)])
+        go("gz", j - 1, dz.at[c, y, z], dz.at[c, y, z], dev_z(j), dz.at[c, y, zb(j)], together=True)
+    all_sent("gz", dz.at[0, 0, pl.ds(0, 7)])
     for i in FAR_Y:
-        go("gy", i - 1, dz.at[c, y, z], dz.at[c, y, z], dev_y(i), dz.at[c, yb(i), z])
+        go("gy", i - 1, dz.at[c, y, z], dz.at[c, y, z], dev_y(i), None, together=True)
+    got("qx", 0)
+    got("qx", 1)
+    got_local(7)
+    tiles = r3[...].astype(F32).reshape(64, 16, 128)
+    top = tiles[:, :8].reshape(512, 128)
+    low = tiles[:, 8:].reshape(512, 128)
+    sq_q = top[:, :64].astype(BF)
+    sq_k = top[:, 64:].astype(BF)
+    sq_v = low[:, :64].astype(BF)
+    kt = top[:, 64:].T.astype(BF)
+    vt = low[:, :64].T.astype(BF)
+
+    def near_rows(ref):
+        return jnp.concatenate([ref[:, (z + i) % 8, c].astype(F32) for i in NEAR_ROWS], axis=0)
+
+    own = near_rows(r3)
+    own_q = own[:, :8].reshape(128, 128)[:, :64].astype(BF)
+    own_v = own[:, 8:].reshape(128, 128)[:, :64].astype(BF)
+    sscale = 1.0 / 64 ** 0.5
+
+    def columns_softmax(scores):
+        weights = jnp.exp(scores - jnp.max(scores, axis=0, keepdims=True))
+        return weights / jnp.sum(weights, axis=0, keepdims=True)
+
+    def attend(probs):
+        high = probs.astype(BF)
+        rounded = nn(vt, high)
+        return rounded, rounded + nn(vt, (probs - high.astype(F32)).astype(BF))
+
+    sprobs = columns_softmax(nt(sq_k, sq_q) * sscale)
+    spt[...] = sprobs.reshape(4, 8, 2, 8, 512)
+    attended, ot[...] = attend(sprobs)
+    att[...] = attended.astype(BF)
+    sprobs = columns_softmax(nt(sq_k, own_q) * sscale)
+    spi[...] = sprobs
+    _, oti[...] = attend(sprobs)
+
     for j in ARRIVE_Z:
         got("gz", j - 1)
         slot = zb(j)
         for i in FAR_Y:
-            go("gy", j * 3 + i - 1, dz.at[c, y, slot], dz.at[c, y, slot], dev_y(i), dz.at[c, yb(i), slot])
-    go("gs", 0, dz.at[c, y], dz.at[c, y], sib, dz.at[1 - c, y])
+            go("gy", i - 1, dz.at[c, y, slot], dz.at[c, y, slot], dev_y(i), None, together=True)
+    all_sent("gy", dz.at[0, pl.ds(0, 3)])
+    go("gs", 0, dz.at[c, y], dz.at[c, y], sib, None, together=True)
     for i in (1, 3, 2):
-        for j in range(8):
-            got("gy", j * 3 + i - 1)
         slot = yb(i)
-        go("gs", i, dz.at[c, slot], dz.at[c, slot], sib, dz.at[1 - c, slot])
-    for i in range(4):
-        got("gs", i)
+        all_here("gy", i - 1, dz.at[c, slot])
+        got("gy", i - 1)
+        go("gs", 0, dz.at[c, slot], dz.at[c, slot], sib, None, together=True)
+    all_here("gs", 0, dz.at[1 - c])
+    all_sent("gs", dz.at[c])
+    got("gs")
 
     got_local(1)
     dz0 = dz[0].reshape(512, 512)
@@ -385,40 +437,54 @@
     gls[...] = jnp.concatenate([jnp.where(first, r[:8], r[8:]) for r in rows], axis=0).astype(BF)
     go("lat", 0, gls, glr, diag, glr, when=swapped)
     local(10, gls, glr, when=kept)
+    leave()
     drain()
 
 
-def finish(pts, or2, glr, pjr, gpts, glat, gqkv, gproj, held, sem):
-    into = pltpu.make_async_copy(pts, held, sem.at[0])
-    into.start()
-    into.wait()
-    out = pltpu.make_async_copy(held, gpts, sem.at[1])
-    out.start()
+def finish(pts_in, or2_in, glr_in, pjr_in, gpts_out, glat_out, gqkv_out, gproj_out,
+           pts, or2, glr, pjr, glat, gqkv, gproj, sem):
+    def copy(i, src, dst):
+        moved = pltpu.make_async_copy(src, dst, sem.at[i])
+        moved.start()
+        return moved
+
+    loads = [copy(0, pts_in, pts), copy(1, pjr_in, pjr), copy(2, glr_in, glr), copy(3, or2_in, or2)]
+    loads[0].wait()
+    stores = [copy(4, pts, gpts_out)]
+    loads[1].wait()
     total = pjr[0].astype(F32)
     for src in (1, 2, 3):
         total = total + pjr[src].astype(F32)
     gproj[...] = total
+    stores.append(copy(5, gproj, gproj_out))
+    loads[2].wait()
     lr = glr[...].astype(F32)
     glat[0] = jnp.concatenate([lr[:8], lr[8:]], axis=1).astype(BF)
+    stores.append(copy(6, glat, glat_out))
+    loads[3].wait()
     res = or2[...].astype(F32).reshape(16, 16, 128)
     parts = [res[h, :8, 0:64] for h in range(16)]
     parts += [res[h, :8, 64:128] for h in range(16)]
     parts += [res[h, 8:, 0:64] for h in range(16)]
     gqkv[0] = jnp.concatenate(parts, axis=1).astype(BF)
-    out.wait()
+    stores.append(copy(7, gqkv, gqkv_out))
+    for moved in stores:
+        moved.wait()
 
 
 def on_device(points, order, cotangent, kv_cross, self_qkv, kv_weight, out_weight):
-    vmem = pl.BlockSpec(memory_space=pltpu.VMEM)
     hbm = pl.BlockSpec(memory_space=pl.ANY)
     scratch = [
+        ((1, 1, 256), jnp.int32),
+        ((1, 8, 2048), BF),
+        ((1, 8, 3072), BF),
         ((256, 1024), BF),
         ((256, 1024), BF),
-        ((256, 1024), BF),
-        ((256, 1024), BF),
+        ((2, 256, 1024), BF),
         ((2, 16, 512), BF),
         ((2, 16, 512), BF),
-        ((2, 4, 8, 16, 1024), BF),
+        ((2, 4, 8, 16, KA), BF),
+        ((2, 4, 8, 16, KB), BF),
         ((16, 16, 128), BF),
         ((4, 4, 16, 128), BF),
         ((4, 8, 16, 128), BF),
@@ -455,10 +521,10 @@
             jax.ShapeDtypeStruct((16, 512), BF),
             jax.ShapeDtypeStruct((4, 16, 1024), BF),
         ),
-        in_specs=[hbm, vmem, hbm, vmem, vmem, hbm, hbm],
+        in_specs=[hbm] * 7,
         out_specs=(hbm, hbm, hbm, hbm),
         scratch_shapes=[pltpu.VMEM(shape, dtype) for shape, dtype in scratch]
-        + [pltpu.SemaphoreType.DMA((COUNT,)), pltpu.SemaphoreType.DMA((COUNT,)), pltpu.SemaphoreType.DMA((14,))],
+        + [pltpu.SemaphoreType.DMA((COUNT,)), pltpu.SemaphoreType.DMA((COUNT,)), pltpu.SemaphoreType.DMA((17,))],
         name="fused_backward",
         cost_estimate=pl.CostEstimate(flops=3_000_000_000, bytes_accessed=8_000_000, transcendentals=400_000),
         compiler_params=pltpu.CompilerParams(
@@ -473,9 +539,18 @@
             jax.ShapeDtypeStruct((1, 8, 3072), BF),
             jax.ShapeDtypeStruct((16, 1024), F32),
         ),
-        in_specs=[hbm, vmem, vmem, vmem],
-        out_specs=(hbm, vmem, vmem, vmem),
-        scratch_shapes=[pltpu.VMEM((1, 256, 1024), BF), pltpu.SemaphoreType.DMA((2,))],
+        in_specs=[hbm] * 4,
+        out_specs=(hbm,) * 4,
+        scratch_shapes=[
+            pltpu.VMEM((1, 256, 1024), BF),
+            pltpu.VMEM((4, 4, 16, 128), BF),
+            pltpu.VMEM((16, 512), BF),
+            pltpu.VMEM((4, 16, 1024), BF),
+            pltpu.VMEM((1, 8, 1024), BF),
+            pltpu.VMEM((1, 8, 3072), BF),
+            pltpu.VMEM((16, 1024), F32),
+            pltpu.SemaphoreType.DMA((8,)),
+        ],
         name="finish",
         cost_estimate=pl.CostEstimate(flops=100_000, bytes_accessed=1_500_000, transcendentals=0),
     )(*parts)

time: 75.4 us -> 72.3 us (0.959); the launches traced: 75.2 us -> 71 us
  Pallas kernels: 74.6 us -> 70.3 us
    pallas_call x1, Pallas kernels: 71.1 us -> 68.4 us  [on_device(): pl.pallas_call(kernel, out_shape=(jax.ShapeDtypeStruct((1, 256, 1024), BF...]
    pallas_call x1, Pallas kernels: 3.46 us -> 1.93 us  [on_device(): pl.pallas_call(finish, out_shape=(jax.ShapeDtypeStruct((1, 256, 1024), BF...]
where the time goes in v3:
time: 72.3 us; the launch traced here: 71 us
  Pallas kernels  70.3 us (97%)
    pallas_call x1, Pallas kernels, on_device(): pl.pallas_call(kernel, out_shape=(jax.ShapeDtypeStruct((1, 256, 1024), BF...  68.4 us
    pallas_call x1, Pallas kernels, on_device(): pl.pallas_call(finish, out_shape=(jax.ShapeDtypeStruct((1, 256, 1024), BF...  1.93 us

profile of v3, /device:TPU:39, one launch (start us, length us, event | category | flops | bytes accessed | tf_op | source)
XLA Modules:
  0.0 71.0 jit_solution(554887346765602931)
XLA Ops:
  0.6 68.4 %fused_backward.1 = (bf16[1,256,1024]{2,1,0:T(8,128)(2,1)}, bf16[4,4,16,128]{3,2,1,0:T(8,128)(2,1)}, bf16[16,512]{1,0:T(8,128)(2,1)}, bf16[4,16,1024]{2,1,0:T(8,128)(2,1)}) custom-call(bf16[1,256,1024]{2,1,0:T(8,128)(2,1)} %points.1, s32[1,1,256]{2,1,0:T(1,128)} %order_in.1, bf16[1,256,1024]{2,1,0:T(8,128)(2,1)} %cot.1, bf16[1,8,2048]{2,1,0:T(8,128)(2,1)} %kv_in.1, ...), custom_call_target="tpu_custom_call" | custom-call | flops 3000000000 | bytes 8000000 | tf_op jit(solution)/shard_map/fused_backward/pallas_call | solution.py:516
  69.0 1.9 %finish.1 = (bf16[1,256,1024]{2,1,0:T(8,128)(2,1)}, bf16[1,8,1024]{2,1,0:T(8,128)(2,1)}, bf16[1,8,3072]{2,1,0:T(8,128)(2,1)}, f32[16,1024]{1,0:T(8,128)}) custom-call(bf16[1,256,1024]{2,1,0:T(8,128)(2,1)} %get-tuple-element.8.pts_in, bf16[4,4,16,128]{3,2,1,0:T(8,128)(2,1)} %get-tuple-element.9.or2_in, bf16[16,512]{1,0:T(8,128)(2,1)} %get-tuple-element.10.glr_in, ...), custom_call_target="tpu_custom_call" | custom-call | flops 100000 | bytes 1500000 | tf_op jit(solution)/shard_map/finish/pallas_call | solution.py:534

commit v4 on v3

--- a/solution.py
+++ b/solution.py
@@ -28,7 +28,7 @@
     kvrow=2, qy=3, qz=7, qx=2, swap_q=1, swap_g=1, kz=7, ky=3, ks=1, kyb=3, kzb=7, ksb=1,
     pair=4, ry=24, rz=7, gz=7, gy=24, gs=4, lat=1, proj=4, back=16, pts=1,
 )
-KA, KB = 768, 256
+KA, KB = 896, 128
 MIX_Z = (4, 1, 7, 2, 6, 3, 5)
 FAR_Z = (4, 3, 5, 2, 6, 1, 7)
 NEAR_Z = (1, 7, 2, 6, 3, 5, 4)
@@ -174,7 +174,8 @@
     head = y * 4 + z4
     local(13, cot.at[0], cotb)
     local(0, wkv, wkvb)
-    local(1, wo.at[pl.ds(pl.multiple_of(head * 64, 64), 64)], wob)
+    for t in (0, 1):
+        local(1 + 16 * t, wo.at[pl.ds(pl.multiple_of(head * 64, 64), 64), pl.ds(t * 512, 512)], wob.at[t])
 
     got_local(14)
     kvw = kv[0].astype(F32)
@@ -222,7 +223,7 @@
     kvb[c, y, z] = right[:, KA - 512:].astype(BF)
     for i in FAR_Y:
         go("ky", i - 1, kv16.at[c, y, z], kv16.at[c, y, z], dev_y(i), None, together=True)
-    for j in MIX_Z:
+    for j in NEAR_Z:
         go("kz", j - 1, kv16.at[c, y, z], kv16.at[c, y, z], dev_z(j), kv16.at[c, y, zb(j)], together=True)
     all_sent("kz", kv16.at[0, 0, pl.ds(0, 7)])
 
@@ -235,7 +236,7 @@
     for i in FAR_Y:
         go("kyb", i - 1, kvb.at[c, y, z], kvb.at[c, y, z], dev_y(i), kvb.at[c, yb(i), z], together=True)
     all_sent("kyb", kvb.at[0, 0, pl.ds(0, 3)])
-    for j in ARRIVE_Z[:4]:
+    for j in NEAR_Z[:4]:
         on_along_y(j)
     for j in (1, 2, 3):
         got("kyb", j - 1)
@@ -243,7 +244,7 @@
         go("kzb", j - 1, kvb.at[c, :, z], kvb.at[c, :, z], dev_z(j), None, rj=0, together=True)
     all_here("kzb", 0, kvb.at[c, :, pl.ds(0, 7)])
     all_sent("kzb", kvb.at[c, :, pl.ds(0, 7)])
-    for j in ARRIVE_Z[4:]:
+    for j in NEAR_Z[4:]:
         on_along_y(j)
     got("qy")
     got_local(3)
@@ -309,9 +310,10 @@
         pown[yi] = nn(pboth[yi], qg[c]).reshape(8, 16, 512)
     all_sent("pair", psend)
     for i in FAR_Y:
-        yi = (y + i) % 4
         got("pair", i)
-        for j in FAR_Z + (0,):
+    for j in FAR_Z + (0,):
+        for i in FAR_Y:
+            yi = (y + i) % 4
             zj = (z + j) % 8
             ysend[j, i - 1] = (pown[yi, zj] + precv[yi, zj].astype(F32)).astype(BF)
             go("ry", j * 3 + i - 1, ysend.at[j, i - 1], yrecv.at[j, i - 1], dev_y(i), yrecv.at[j, i - 1], together=True)
@@ -338,7 +340,7 @@
         acc = acc + zrecv[j - 1].astype(F32)
     dz[c, y, z] = acc.astype(BF)
 
-    for j in MIX_Z:
+    for j in NEAR_Z:
         go("gz", j - 1, dz.at[c, y, z], dz.at[c, y, z], dev_z(j), dz.at[c, y, zb(j)], together=True)
     all_sent("gz", dz.at[0, 0, pl.ds(0, 7)])
     for i in FAR_Y:
@@ -380,7 +382,7 @@
     spi[...] = sprobs
     _, oti[...] = attend(sprobs)
 
-    for j in ARRIVE_Z:
+    for j in NEAR_Z:
         got("gz", j - 1)
         slot = zb(j)
         for i in FAR_Y:
@@ -394,12 +396,14 @@
         go("gs", 0, dz.at[c, slot], dz.at[c, slot], sib, None, together=True)
     all_here("gs", 0, dz.at[1 - c])
     all_sent("gs", dz.at[c])
+    got_local(1)
+    got_local(17)
+    datt = nt(dz[c].reshape(512, 512), wob[c])
     got("gs")
 
-    got_local(1)
     dz0 = dz[0].reshape(512, 512)
     dz1 = dz[1].reshape(512, 512)
-    datt = nt(dz0, wob[:, 0:512]) + nt(dz1, wob[:, 512:1024])
+    datt = datt + nt(dz[1 - c].reshape(512, 512), wob[1 - c])
     datt = datt.astype(BF)
     dattw = datt.astype(F32)
     dat[...] = dattw.reshape(4, 8, 2, 8, 64)
@@ -490,7 +494,7 @@
         ((4, 8, 16, 128), BF),
         ((4, 8, 2, 16, 128), BF),
         ((1024, 2048), BF),
-        ((64, 1024), BF),
+        ((2, 64, 512), BF),
         ((2, 512, 512), BF),
         ((4, 8, 2, 8, 512), F32),
         ((512, 128), F32),
@@ -524,7 +528,7 @@
         in_specs=[hbm] * 7,
         out_specs=(hbm, hbm, hbm, hbm),
         scratch_shapes=[pltpu.VMEM(shape, dtype) for shape, dtype in scratch]
-        + [pltpu.SemaphoreType.DMA((COUNT,)), pltpu.SemaphoreType.DMA((COUNT,)), pltpu.SemaphoreType.DMA((17,))],
+        + [pltpu.SemaphoreType.DMA((COUNT,)), pltpu.SemaphoreType.DMA((COUNT,)), pltpu.SemaphoreType.DMA((18,))],
         name="fused_backward",
         cost_estimate=pl.CostEstimate(flops=3_000_000_000, bytes_accessed=8_000_000, transcendentals=400_000),
         compiler_params=pltpu.CompilerParams(

time: 72.3 us -> 69.5 us (0.961); the launches traced: 71 us -> 69.4 us
  Pallas kernels: 70.3 us -> 68.7 us
    pallas_call x1, Pallas kernels: 68.4 us -> 66.8 us  [on_device(): pl.pallas_call(kernel, out_shape=(jax.ShapeDtypeStruct((1, 256, 1024), BF...]
where the time goes in v4:
time: 69.5 us; the launch traced here: 69.4 us
  Pallas kernels  68.7 us (99%)
    pallas_call x1, Pallas kernels, on_device(): pl.pallas_call(kernel, out_shape=(jax.ShapeDtypeStruct((1, 256, 1024), BF...  66.8 us
    pallas_call x1, Pallas kernels, on_device(): pl.pallas_call(finish, out_shape=(jax.ShapeDtypeStruct((1, 256, 1024), BF...  1.93 us

profile of v4, /device:TPU:39, one launch (start us, length us, event | category | flops | bytes accessed | tf_op | source)
XLA Modules:
  0.0 69.4 jit_solution(1841778768419889236)
XLA Ops:
  0.6 66.8 %fused_backward.1 = (bf16[1,256,1024]{2,1,0:T(8,128)(2,1)}, bf16[4,4,16,128]{3,2,1,0:T(8,128)(2,1)}, bf16[16,512]{1,0:T(8,128)(2,1)}, bf16[4,16,1024]{2,1,0:T(8,128)(2,1)}) custom-call(bf16[1,256,1024]{2,1,0:T(8,128)(2,1)} %points.1, s32[1,1,256]{2,1,0:T(1,128)} %order_in.1, bf16[1,256,1024]{2,1,0:T(8,128)(2,1)} %cot.1, bf16[1,8,2048]{2,1,0:T(8,128)(2,1)} %kv_in.1, ...), custom_call_target="tpu_custom_call" | custom-call | flops 3000000000 | bytes 8000000 | tf_op jit(solution)/shard_map/fused_backward/pallas_call | solution.py:520
  67.4 1.9 %finish.1 = (bf16[1,256,1024]{2,1,0:T(8,128)(2,1)}, bf16[1,8,1024]{2,1,0:T(8,128)(2,1)}, bf16[1,8,3072]{2,1,0:T(8,128)(2,1)}, f32[16,1024]{1,0:T(8,128)}) custom-call(bf16[1,256,1024]{2,1,0:T(8,128)(2,1)} %get-tuple-element.8.pts_in, bf16[4,4,16,128]{3,2,1,0:T(8,128)(2,1)} %get-tuple-element.9.or2_in, bf16[16,512]{1,0:T(8,128)(2,1)} %get-tuple-element.10.glr_in, ...), custom_call_target="tpu_custom_call" | custom-call | flops 100000 | bytes 1500000 | tf_op jit(solution)/shard_map/finish/pallas_call | solution.py:538

commit v5 on v4

--- a/solution.py
+++ b/solution.py
@@ -151,7 +151,7 @@
     greet = [sib, dev(xlo, 1 - c, y, z, 1 - xhi), dev(xlo, c, y, z, 1 - xhi)]
     greet += [dev_y(j) for j in (1, 2, 3)] + [dev_z(j) for j in range(1, 8)]
     greet += [back_to(j, i) for j in range(4) for i in range(8) if i in NEAR_ROWS + (6,) and (j, i) != (0, 0)]
-    for to in greet:
+    for to in reversed(greet):
         pl.semaphore_signal(barrier, inc=1, device_id=to, device_id_type=MESH)
 
     def far(a, t):
@@ -301,14 +301,19 @@
     ds = (p * (dp - delta) * scale).astype(BF)
     pboth[...] = jnp.concatenate([ds, p.astype(BF)], axis=1).reshape(4, 128, 512)
 
-    for i in FAR_Y + (0,):
+    def for_sibling(i):
         yi = (y + i) % 4
         psend[yi] = nn(pboth[yi], qg[1 - c]).astype(BF).reshape(8, 16, 512)
         go("pair", i, psend.at[yi], precv.at[yi], sib, precv.at[yi], together=True)
-    for i in FAR_Y + (0,):
+
+    def for_own(i):
         yi = (y + i) % 4
         pown[yi] = nn(pboth[yi], qg[c]).reshape(8, 16, 512)
-    all_sent("pair", psend)
+
+    for i in FAR_Y:
+        for_sibling(i)
+    for i in FAR_Y:
+        for_own(i)
     for i in FAR_Y:
         got("pair", i)
     for j in FAR_Z + (0,):
@@ -317,6 +322,9 @@
             zj = (z + j) % 8
             ysend[j, i - 1] = (pown[yi, zj] + precv[yi, zj].astype(F32)).astype(BF)
             go("ry", j * 3 + i - 1, ysend.at[j, i - 1], yrecv.at[j, i - 1], dev_y(i), yrecv.at[j, i - 1], together=True)
+    for_sibling(0)
+    for_own(0)
+    all_sent("pair", psend)
     all_sent("ry", ysend)
 
     gps[:, 0:KA] = tn(ds, kv16[0].reshape(512, KA)).astype(BF)

time: 69.5 us -> 69.3 us (level)
  no operation moved by 1% of the time
where the time goes in v5:
time: 69.3 us; the launch traced here: 69.2 us
  Pallas kernels  68.6 us (99%)
    pallas_call x1, Pallas kernels, on_device(): pl.pallas_call(kernel, out_shape=(jax.ShapeDtypeStruct((1, 256, 1024), BF...  66.7 us
    pallas_call x1, Pallas kernels, on_device(): pl.pallas_call(finish, out_shape=(jax.ShapeDtypeStruct((1, 256, 1024), BF...  1.93 us

profile of v5, /device:TPU:39, one launch (start us, length us, event | category | flops | bytes accessed | tf_op | source)
XLA Modules:
  0.0 69.2 jit_solution(9140415959206762648)
XLA Ops:
  0.6 66.7 %fused_backward.1 = (bf16[1,256,1024]{2,1,0:T(8,128)(2,1)}, bf16[4,4,16,128]{3,2,1,0:T(8,128)(2,1)}, bf16[16,512]{1,0:T(8,128)(2,1)}, bf16[4,16,1024]{2,1,0:T(8,128)(2,1)}) custom-call(bf16[1,256,1024]{2,1,0:T(8,128)(2,1)} %points.1, s32[1,1,256]{2,1,0:T(1,128)} %order_in.1, bf16[1,256,1024]{2,1,0:T(8,128)(2,1)} %cot.1, bf16[1,8,2048]{2,1,0:T(8,128)(2,1)} %kv_in.1, ...), custom_call_target="tpu_custom_call" | custom-call | flops 3000000000 | bytes 8000000 | tf_op jit(solution)/shard_map/fused_backward/pallas_call | solution.py:528
  67.3 1.9 %finish.1 = (bf16[1,256,1024]{2,1,0:T(8,128)(2,1)}, bf16[1,8,1024]{2,1,0:T(8,128)(2,1)}, bf16[1,8,3072]{2,1,0:T(8,128)(2,1)}, f32[16,1024]{1,0:T(8,128)}) custom-call(bf16[1,256,1024]{2,1,0:T(8,128)(2,1)} %get-tuple-element.8.pts_in, bf16[4,4,16,128]{3,2,1,0:T(8,128)(2,1)} %get-tuple-element.9.or2_in, bf16[16,512]{1,0:T(8,128)(2,1)} %get-tuple-element.10.glr_in, ...), custom_call_target="tpu_custom_call" | custom-call | flops 100000 | bytes 1500000 | tf_op jit(solution)/shard_map/finish/pallas_call | solution.py:546
